TPU v7x, 256 devices: a whole 4x4x8 slice. The times are simulated.
256 devices in a mesh: scen: 8 (over z), blk: 32 (over x, y, core).
Axes of the slice: x: 4, y: 4, z: 8, core: 2. Of those that a mesh axis runs over, the one named last changes fastest.
Arguments:
- local_tiles: bfloat16 [7168, 128, 128], P('blk'), may hold values from -0.1875 to 0.1875
- local_rows: int32 [7168], P('blk'), may hold values from 0 to 39
- local_cols: int32 [7168], P('blk'), may hold values from 0 to 31
- far_tiles: bfloat16 [1024, 1, 128, 128], P('blk'), may hold values from -0.375 to 0.375
- far_rows: int32 [1024, 1], P('blk'), may hold values from 0 to 39
- far_cols: int32 [1024, 1], P('blk'), may hold values from 0 to 31
- link_tiles: bfloat16 [4096, 128, 128], P(('scen', 'blk')), may hold values from -0.5 to 0.5
- link_rows: int32 [4096], P(('scen', 'blk')), may hold values from 0 to 39
- link_cols: int32 [4096], P(('scen', 'blk')), may hold values from 0 to 15
- inflows: bfloat16 [256, 163840], P('scen', 'blk'), may hold values from -6 to 6
- recourse_cost: float32 [131072], P('blk'), may hold values from -6 to 6
- first_cost: float32 [2048], P('scen'), may hold values from -6 to 6
- first_section: float32 [2048], P('scen'), may hold values from 0 to 2
- recourse: float32 [256, 131072], P('scen', 'blk'), may hold values from 0 to 2
- duals: float32 [256, 163840], P('scen', 'blk'), may hold values from -6 to 6
Outputs:
- first_out: float32 [2048], P('scen')
- recourse_out: float32 [256, 131072], P('scen', 'blk')
- duals_out: float32 [256, 163840], P('scen', 'blk')
Inputs may be any that keep to these rules, and one draw needn't show every extreme that they name: `far_cols`: far tile entry (b * (blk size) + p, k) lies in a row block owned by blk index b and in a column block owned by blk index p; every blk index holds exactly 1 far tiles for every blk index, its own included. `far_rows`: row offsets count within the row blocks of the holding blk index. Linking tiles of device (g, b) lie in row blocks owned by b; link_cols names a block of 128 first-section columns.
All inputs are finite; a program needn't handle non-finite values.
Results may differ from a plain program's by a relative error of at most 0.017.
Values may be sent and summed in bfloat16 or wider, within the bound.
A program may use at most 64 MiB of HBM per device.

v0:
```python
import jax
import jax.numpy as jnp
from jax import lax
from jax.sharding import PartitionSpec as P

TILE = 128
ITERS = 2


primal_stepsize = 0.4
first_step = 2.0
dual_step = 0.4


def one_hot(index_set, count):
    return (index_set[..., None] == jnp.arange(count, dtype=jnp.int32)).astype(jnp.float32)


def body(
    local_tiles,
    local_rows,
    local_cols,
    far_tiles,
    far_rows,
    far_cols,
    link_tiles,
    link_rows,
    link_cols,
    inflows,
    recourse_cost,
    first_cost,
    first_section,
    recourse,
    duals,
):
    scen_groups = lax.axis_size("scen")
    scenarios = duals.shape[0]
    row_blocks = duals.shape[1] // TILE
    col_blocks = recourse.shape[1] // TILE
    first_blocks = first_cost.shape[0] * scen_groups // TILE
    total_scen = scenarios * scen_groups
    nearby_row_onehot = one_hot(local_rows, row_blocks)
    local_col_hot = one_hot(local_cols, col_blocks)
    distant_row_onehot = one_hot(far_rows, row_blocks)
    link_row_hot = one_hot(link_rows, row_blocks)
    link_first_hot = one_hot(link_cols, first_blocks)
    wanted = lax.all_to_all(far_cols, "blk", split_axis=0, concat_axis=0, tiled=True)
    wanted_hot = one_hot(wanted, col_blocks)
    first_full, cost_full = (
        lax.all_gather(first_section, "scen", axis=0, tiled=True),
        lax.all_gather(first_cost, "scen", axis=0, tiled=True),
    )
    for step in range(ITERS):
        half = duals.astype(jnp.bfloat16).reshape(scenarios, row_blocks, TILE)
        far_half = jnp.take(half, far_rows, axis=1)
        partial_value = jnp.einsum(
            "spkr,pkrc->spkc", far_half, far_tiles, preferred_element_type=jnp.float32
        )
        far_terms = lax.all_to_all(partial_value, "blk", split_axis=1, concat_axis=1, tiled=True)
        link_half = jnp.take(half, link_rows, axis=1)
        link_terms = jnp.einsum(
            "snr,nrc->nc", link_half, link_tiles, preferred_element_type=jnp.float32
        )
        first_part = jnp.einsum("nc,nb->bc", link_terms, link_first_hot)
        first_grad = lax.psum(first_part, ("scen", "blk")).reshape(-1)
        first_new = jnp.maximum(
            first_full - first_step * (cost_full - first_grad / total_scen), 0.0
        )
        first_bar = (2.0 * first_new - first_full).astype(jnp.bfloat16)
        first_full = first_new
        picked = jnp.take(half, local_rows, axis=1)
        local_terms = jnp.einsum(
            "snr,nrc->snc", picked, local_tiles, preferred_element_type=jnp.float32
        )
        recourse_gradient = jnp.einsum("snc,nb->sbc", local_terms, local_col_hot)
        recourse_gradient = recourse_gradient + jnp.einsum("sqkc,qkb->sbc", far_terms, wanted_hot)
        recourse_new = jnp.maximum(
            recourse
            - primal_stepsize * (recourse_cost[None, :] - recourse_gradient.reshape(scenarios, -1)),
            0.0,
        )
        extrapolated = (
            (2.0 * recourse_new - recourse)
            .astype(jnp.bfloat16)
            .reshape(scenarios, col_blocks, TILE)
        )
        recourse = recourse_new
        sent = jnp.take(extrapolated, wanted, axis=1)
        came = lax.all_to_all(sent, "blk", split_axis=1, concat_axis=1, tiled=True)
        picked_cols = jnp.take(extrapolated, local_cols, axis=1)
        forward_products = jnp.einsum(
            "snc,nrc->snr", picked_cols, local_tiles, preferred_element_type=jnp.float32
        )
        matrix_image = jnp.einsum("yhf,hj->yjf", forward_products, nearby_row_onehot)
        first_pieces = jnp.take(first_bar.reshape(first_blocks, TILE), link_cols, axis=0)
        link_image = jnp.einsum(
            "nc,nrc->nr", first_pieces, link_tiles, preferred_element_type=jnp.float32
        )
        matrix_image = matrix_image + jnp.einsum("nr,nb->br", link_image, link_row_hot)[None]
        distant_image = jnp.einsum(
            "spkc,pkrc->spkr", came, far_tiles, preferred_element_type=jnp.float32
        )
        matrix_image = matrix_image + jnp.einsum("cjox,joi->cix", distant_image, distant_row_onehot)
        duals = duals + dual_step * (
            inflows.astype(jnp.float32) - matrix_image.reshape(scenarios, -1)
        )
    own_length = first_section.shape[0]
    own_first = lax.dynamic_slice_in_dim(
        first_full, lax.axis_index("scen") * own_length, own_length
    )
    return (own_first, recourse, duals)


def solution(mesh):
    in_specs = (
        P("blk", None, None),
        P("blk"),
        P("blk"),
        P("blk", None, None, None),
        P("blk", None),
        P("blk", None),
        P(("scen", "blk"), None, None),
        P(("scen", "blk")),
        P(("scen", "blk")),
        P("scen", "blk"),
        P("blk"),
        P("scen"),
        P("scen"),
        P("scen", "blk"),
        P("scen", "blk"),
    )
    out_specs = (P("scen"), P("scen", "blk"), P("scen", "blk"))
    return jax.shard_map(body, mesh=mesh, in_specs=in_specs, out_specs=out_specs, check_vma=False)
```

profile of v0, /device:TPU:1, one launch (start us, length us, event | category | flops | bytes accessed | tf_op | source)
XLA Modules:
  0.0 304.9 jit_solution(4662607954259255618)
XLA Ops:
  0.7 1.4 copy.70
  2.1 8.6 %all-to-all-start = ((s32[32,1,1]{2,1,0:T(1,128)}), s32[32,1,1]{2,1,0:T(1,128)S(1)}, u32[]{:S(2)}, u32[]{:S(2)}) async-start(s32[32,1,1]{2,1,0:T(1,128)} %copy.70), calls=%async_computation | async-start | bytes 32768 | tf_op jit(solution)/shard_map/all_to_all | solution.py:47
  17.4 15.6 %all-gather = f32[8,1,256]{2,1,0:T(1,128)S(1)} all-gather(f32[1,1,256]{2,1,0:T(1,128)} %bitcast.301), channel_id=1, replica_groups=mesh['scen'=8,'blk'=32] {'scen'}, dimensions={0}, use_global_device_ids=true | all-gather | bytes 9216 | tf_op jit(solution)/shard_map/all_gather | solution.py:50
  33.0 10.1 %all-gather.1 = f32[8,1,256]{2,1,0:T(1,128)S(1)} all-gather(f32[1,1,256]{2,1,0:T(1,128)} %bitcast.302), channel_id=1, replica_groups=mesh['scen'=8,'blk'=32] {'scen'}, dimensions={0}, use_global_device_ids=true | all-gather | bytes 9216 | tf_op jit(solution)/shard_map/all_gather | solution.py:51
  43.1 1.1 copy_bitcast_fusion.1
  45.6 1.3 fusion.129
  47.1 81.6 %psum.14 = f32[16,128]{1,0:T(8,128)S(1)} all-reduce(f32[16,128]{1,0:T(8,128)S(1)} %fusion.113), channel_id=1, replica_groups=mesh['scen'=8,'blk'=32] {'scen','blk'}, use_global_device_ids=true, to_apply=%region_1.3 | all-reduce | flops 2048 | bytes 16384 | tf_op jit(solution)/shard_map/psum | solution.py:65
  130.0 2.1 gather_fusion.1
  134.1 1.2 convolution_bitcast_fusion.7
  135.2 5.7 %convolution_bitcast_fusion.3 = bf16[32,224,128]{2,0,1:T(8,128)(2,1)S(1)} fusion(bf16[224,128,128]{2,1,0:T(8,128)(2,1)} %param.27, bf16[224,32,128]{2,1,0:T(8,128)(2,1)} %gather_fusion.1, pred[224]{0:T(512)(128)(4,1)S(1)} %compare_and_fusion.2), kind=kOutput, calls=%fused_computation.23 | convolution fusion | flops 235798528 | bytes 11010272 | tf_op jit(solution)/shard_map/snr,nrc->snc/dot_general | solution.py:72
  141.0 4.9 %all-to-all-start.1 = ((bf16[32,32,1,128]{3,0,2,1:T(8,128)(2,1)}), bf16[32,32,1,128]{3,0,2,1:T(8,128)(2,1)}, u32[]{:S(2)}, u32[]{:S(2)}) async-start(bf16[32,32,1,128]{3,0,2,1:T(8,128)(2,1)} %convolution_bitcast_fusion.7), calls=%async_computation.1 | async-start | bytes 524288 | tf_op jit(solution)/shard_map/all_to_all | solution.py:59
  146.6 8.4 %all-to-all-done.1 = bf16[32,32,1,128]{3,0,2,1:T(8,128)(2,1)} async-done(((bf16[32,32,1,128]{3,0,2,1:T(8,128)(2,1)}), bf16[32,32,1,128]{3,0,2,1:T(8,128)(2,1)}, u32[]{:S(2)}, u32[]{:S(2)}) %all-to-all-start.1) | async-done | bytes 262176 | tf_op jit(solution)/shard_map/all_to_all | solution.py:59
  155.0 1.2 fusion.58
  159.6 4.6 %all-to-all-start.2 = ((bf16[32,32,1,128]{3,0,2,1:T(8,128)(2,1)}), bf16[32,32,1,128]{3,0,2,1:T(8,128)(2,1)}, u32[]{:S(2)}, u32[]{:S(2)}) async-start(bf16[32,32,1,128]{3,0,2,1:T(8,128)(2,1)} %fusion.71), calls=%async_computation.2 | async-start | bytes 524288 | tf_op jit(solution)/shard_map/all_to_all | solution.py:89
  164.1 2.1 gather_fusion.3
  166.3 7.6 %convolution_bitcast_fusion.2 = bf16[32,224,128]{2,0,1:T(8,128)(2,1)S(1)} fusion(bf16[224,128,128]{2,1,0:T(8,128)(2,1)} %param.27, bf16[224,32,128]{2,1,0:T(8,128)(2,1)} %gather_fusion.3, pred[224]{0:T(512)(128)(4,1)S(1)} %compare_and_fusion.1), kind=kOutput, calls=%fused_computation.22 | convolution fusion | flops 235798528 | bytes 11010272 | tf_op jit(solution)/shard_map/snc,nrc->snr/dot_general | solution.py:91
  173.9 1.6 convolution_bitcast_fusion.6
  178.3 1.4 gather_fusion.8
  179.8 2.2 gather_fusion.7
  183.2 0.9 fusion.112
  184.1 75.8 %psum.15 = f32[16,128]{1,0:T(8,128)S(1)} all-reduce(f32[16,128]{1,0:T(8,128)S(1)} %fusion.112), channel_id=1, replica_groups=mesh['scen'=8,'blk'=32] {'scen','blk'}, use_global_device_ids=true, to_apply=%region_3.10 | all-reduce | flops 2048 | bytes 16384 | tf_op jit(solution)/shard_map/psum | solution.py:65
  260.6 2.1 convolution_bitcast_fusion.5
  262.7 5.0 %all-to-all-start.3 = ((bf16[32,32,1,128]{3,0,2,1:T(8,128)(2,1)}), bf16[32,32,1,128]{3,0,2,1:T(8,128)(2,1)}, u32[]{:S(2)}, u32[]{:S(2)}) async-start(bf16[32,32,1,128]{3,0,2,1:T(8,128)(2,1)} %convolution_bitcast_fusion.5), calls=%async_computation.3 | async-start | bytes 524288 | tf_op jit(solution)/shard_map/all_to_all | solution.py:59
  267.8 6.4 %convolution_bitcast_fusion.1 = bf16[32,224,128]{2,0,1:T(8,128)(2,1)} fusion(bf16[224,128,128]{2,1,0:T(8,128)(2,1)} %param.27, bf16[224,32,128]{2,1,0:T(8,128)(2,1)S(1)} %copy-done.2, pred[224]{0:T(512)(128)(4,1)S(1)} %copy-done.33), kind=kOutput, calls=%fused_computation.21 | convolution fusion | flops 235798528 | bytes 11010272 | tf_op jit(solution)/shard_map/snr,nrc->snc/dot_general | solution.py:72
  276.9 1.2 fusion.56
  278.0 2.2 fusion.35
  280.2 1.6 fusion.67
  282.7 2.3 gather_fusion.9
  285.8 7.0 %all-to-all-start.4 = ((bf16[32,32,1,128]{3,0,2,1:T(8,128)(2,1)}), bf16[32,32,1,128]{3,0,2,1:T(8,128)(2,1)S(1)}, u32[]{:S(2)}, u32[]{:S(2)}) async-start(bf16[32,32,1,128]{3,0,2,1:T(8,128)(2,1)} %fusion.68), calls=%async_computation.4 | async-start | bytes 524288 | tf_op jit(solution)/shard_map/all_to_all | solution.py:89
  292.8 7.6 %convolution_bitcast_fusion = bf16[32,224,128]{2,0,1:T(8,128)(2,1)S(1)} fusion(bf16[224,128,128]{2,1,0:T(8,128)(2,1)} %param.27, bf16[224,32,128]{2,1,0:T(8,128)(2,1)} %gather_fusion.9, pred[224]{0:T(512)(128)(4,1)S(1)} %copy-done.31), kind=kOutput, calls=%fused_computation.20 | convolution fusion | flops 235798528 | bytes 11010272 | tf_op jit(solution)/shard_map/snc,nrc->snr/dot_general | solution.py:91
  300.4 1.3 all-to-all-done.4
  303.8 1.1 fusion.49
  (139 shorter events, 26.2 us)
Async XLA Ops:
  0.6 133.4 %copy-start = (bf16[32,1,128,128]{3,2,1,0:T(8,128)(2,1)S(1)}, bf16[32,1,128,128]{3,2,1,0:T(8,128)(2,1)}, u32[]{:S(2)}) copy-start(bf16[32,1,128,128]{3,2,1,0:T(8,128)(2,1)} %param.30) | copy-start | bytes 3145732
  0.6 46.2 %copy-start.40 = (s32[16]{0:T(128)S(1)}, s32[16]{0:T(128)}, u32[]{:S(2)}) copy-start(s32[16]{0:T(128)} %param.35) | copy-start | bytes 196
  2.1 138.9 %all-to-all-start = ((s32[32,1,1]{2,1,0:T(1,128)}), s32[32,1,1]{2,1,0:T(1,128)S(1)}, u32[]{:S(2)}, u32[]{:S(2)}) async-start(s32[32,1,1]{2,1,0:T(1,128)} %copy.70), calls=%async_computation | async-start | bytes 32768 | tf_op jit(solution)/shard_map/all_to_all | solution.py:47
  12.0 33.6 %copy-start.35 = (pred[16]{0:T(512)(128)(4,1)}, pred[16]{0:T(512)(128)(4,1)S(1)}, u32[]{:S(2)}) copy-start(pred[16]{0:T(512)(128)(4,1)S(1)} %compare_and_fusion.3) | copy-start | bytes 52
  13.3 120.7 %copy-start.34 = (pred[32]{0:T(512)(128)(4,1)}, pred[32]{0:T(512)(128)(4,1)S(1)}, u32[]{:S(2)}) copy-start(pred[32]{0:T(512)(128)(4,1)S(1)} %and_bitcast_fusion.1) | copy-start | bytes 100
  14.7 120.5 %copy-start.32 = (pred[224]{0:T(512)(128)(4,1)}, pred[224]{0:T(512)(128)(4,1)S(1)}, u32[]{:S(2)}) copy-start(pred[224]{0:T(512)(128)(4,1)S(1)} %compare_and_fusion.2) | copy-start | bytes 676
  16.1 150.2 %copy-start.30 = (pred[224]{0:T(512)(128)(4,1)}, pred[224]{0:T(512)(128)(4,1)S(1)}, u32[]{:S(2)}) copy-start(pred[224]{0:T(512)(128)(4,1)S(1)} %compare_and_fusion.1) | copy-start | bytes 676
  17.4 115.9 %copy-start.38 = (pred[16]{0:T(512)(128)(4,1)}, pred[16]{0:T(512)(128)(4,1)S(1)}, u32[]{:S(2)}) copy-start(pred[16]{0:T(512)(128)(4,1)S(1)} %compare_and_fusion) | copy-start | bytes 52
  130.0 3.5 %copy-start.1 = (bf16[16,128,128]{2,1,0:T(8,128)(2,1)S(1)}, bf16[16,128,128]{2,1,0:T(8,128)(2,1)}, u32[]{:S(2)}) copy-start(bf16[16,128,128]{2,1,0:T(8,128)(2,1)} %param.33) | copy-start | bytes 1572868
  130.0 3.8 %copy-start.41 = (s32[16]{0:T(128)S(1)}, s32[16]{0:T(128)}, u32[]{:S(2)}) copy-start(s32[16]{0:T(128)} %param.34) | copy-start | bytes 196
  132.1 32.0 %copy-start.20 = (s32[1024]{0:T(1024)}, s32[1024]{0:T(1024)S(1)}, u32[]{:S(2)}) copy-start(s32[1024]{0:T(1024)S(1)} %pad_clamp_fusion.2) | copy-start | bytes 12292
  135.2 21.0 %copy-start.16 = (s32[224]{0:T(256)S(1)}, s32[224]{0:T(256)}, u32[]{:S(2)}) copy-start(s32[224]{0:T(256)} %param.29) | copy-start | bytes 2692
  141.0 14.0 %all-to-all-start.1 = ((bf16[32,32,1,128]{3,0,2,1:T(8,128)(2,1)}), bf16[32,32,1,128]{3,0,2,1:T(8,128)(2,1)}, u32[]{:S(2)}, u32[]{:S(2)}) async-start(bf16[32,32,1,128]{3,0,2,1:T(8,128)(2,1)} %convolution_bitcast_fusion.7), calls=%async_computation.1 | async-start | bytes 524288 | tf_op jit(solution)/shard_map/all_to_all | solution.py:59
  146.5 10.4 %copy-start.26 = (s32[32]{0:T(128)}, s32[32]{0:T(128)S(1)}, u32[]{:S(2)}) copy-start(s32[32]{0:T(128)S(1)} %reduce) | copy-start | bytes 388
  146.5 11.6 %copy-start.24 = (s32[1024]{0:T(1024)}, s32[1024]{0:T(1024)S(1)}, u32[]{:S(2)}) copy-start(s32[1024]{0:T(1024)S(1)} %pad_clamp_fusion) | copy-start | bytes 12292
  146.6 12.2 %copy-start.36 = (pred[32]{0:T(512)(128)(4,1)}, pred[32]{0:T(512)(128)(4,1)S(1)}, u32[]{:S(2)}) copy-start(pred[32]{0:T(512)(128)(4,1)S(1)} %and_bitcast_fusion) | copy-start | bytes 100
  146.6 11.1 %copy-start.14 = (f32[4096]{0:T(1024)S(1)}, f32[4096]{0:T(1024)}, u32[]{:S(2)}) copy-start(f32[4096]{0:T(1024)} %param.37) | copy-start | bytes 49156
  159.6 14.3 %all-to-all-start.2 = ((bf16[32,32,1,128]{3,0,2,1:T(8,128)(2,1)}), bf16[32,32,1,128]{3,0,2,1:T(8,128)(2,1)}, u32[]{:S(2)}, u32[]{:S(2)}) async-start(bf16[32,32,1,128]{3,0,2,1:T(8,128)(2,1)} %fusion.71), calls=%async_computation.2 | async-start | bytes 524288 | tf_op jit(solution)/shard_map/all_to_all | solution.py:89
  166.3 9.2 %copy-start.28 = (s32[32,1]{0,1:T(1,128)S(1)}, s32[32,1]{0,1:T(1,128)}, u32[]{:S(2)}) copy-start(s32[32,1]{0,1:T(1,128)} %param.31) | copy-start | bytes 388
  182.0 85.7 %copy-start.2 = (bf16[224,32,128]{2,1,0:T(8,128)(2,1)S(1)}, bf16[224,32,128]{2,1,0:T(8,128)(2,1)}, u32[]{:S(2)}) copy-start(bf16[224,32,128]{2,1,0:T(8,128)(2,1)} %gather_fusion.7) | copy-start | bytes 5505028
  182.9 84.8 %copy-start.33 = (pred[224]{0:T(512)(128)(4,1)S(1)}, pred[224]{0:T(512)(128)(4,1)}, u32[]{:S(2)}) copy-start(pred[224]{0:T(512)(128)(4,1)} %copy-done.32) | copy-start | bytes 676
  262.7 14.2 %all-to-all-start.3 = ((bf16[32,32,1,128]{3,0,2,1:T(8,128)(2,1)}), bf16[32,32,1,128]{3,0,2,1:T(8,128)(2,1)}, u32[]{:S(2)}, u32[]{:S(2)}) async-start(bf16[32,32,1,128]{3,0,2,1:T(8,128)(2,1)} %convolution_bitcast_fusion.5), calls=%async_computation.3 | async-start | bytes 524288 | tf_op jit(solution)/shard_map/all_to_all | solution.py:59
  267.7 7.2 %copy-start.39 = (pred[16]{0:T(512)(128)(4,1)S(1)}, pred[16]{0:T(512)(128)(4,1)}, u32[]{:S(2)}) copy-start(pred[16]{0:T(512)(128)(4,1)} %copy-done.38) | copy-start | bytes 52
  267.7 8.2 %copy-start.42 = (s32[16]{0:T(128)S(1)}, s32[16]{0:T(128)}, u32[]{:S(2)}) copy-start(s32[16]{0:T(128)} %param.34) | copy-start | bytes 196
  267.7 9.1 %copy-start.27 = (s32[32]{0:T(128)S(1)}, s32[32]{0:T(128)}, u32[]{:S(2)}) copy-start(s32[32]{0:T(128)} %copy-done.26) | copy-start | bytes 388
  267.8 10.3 %copy-start.17 = (s32[224]{0:T(256)S(1)}, s32[224]{0:T(256)}, u32[]{:S(2)}) copy-start(s32[224]{0:T(256)} %param.29) | copy-start | bytes 2692
  276.2 4.0 %copy-start.8 = (f32[32,32,128]{2,0,1:T(8,128)S(1)}, f32[32,32,128]{2,0,1:T(8,128)}, u32[]{:S(2)}) copy-start(f32[32,32,128]{2,0,1:T(8,128)} %copy-done.7) | copy-start | bytes 1572868
  276.2 4.0 %copy-start.10 = (f32[32,4096]{1,0:T(8,128)S(1)}, f32[32,4096]{1,0:T(8,128)}, u32[]{:S(2)}) copy-start(f32[32,4096]{1,0:T(8,128)} %param.40) | copy-start | bytes 1572868
  276.2 4.0 %copy-start.15 = (f32[4096]{0:T(1024)S(1)}, f32[4096]{0:T(1024)}, u32[]{:S(2)}) copy-start(f32[4096]{0:T(1024)} %param.37) | copy-start | bytes 49156
  282.6 10.1 %copy-start.31 = (pred[224]{0:T(512)(128)(4,1)S(1)}, pred[224]{0:T(512)(128)(4,1)}, u32[]{:S(2)}) copy-start(pred[224]{0:T(512)(128)(4,1)} %copy-done.30) | copy-start | bytes 676
  285.8 16.0 %all-to-all-start.4 = ((bf16[32,32,1,128]{3,0,2,1:T(8,128)(2,1)}), bf16[32,32,1,128]{3,0,2,1:T(8,128)(2,1)S(1)}, u32[]{:S(2)}, u32[]{:S(2)}) async-start(bf16[32,32,1,128]{3,0,2,1:T(8,128)(2,1)} %fusion.68), calls=%async_computation.4 | async-start | bytes 524288 | tf_op jit(solution)/shard_map/all_to_all | solution.py:89
  292.8 9.6 %copy-start.29 = (s32[32,1]{0,1:T(1,128)S(1)}, s32[32,1]{0,1:T(1,128)}, u32[]{:S(2)}) copy-start(s32[32,1]{0,1:T(1,128)} %param.31) | copy-start | bytes 388
  (16 other events, 26.2 us)
where the time goes:
time: 306 us; the launch traced here: 305 us
  blocking collectives  183 us (60%)
  matrix products  44.1 us (14%)
  starting transfers between devices  30 us (10%)
  local copies, waits for them, and re-layouts  20.6 us (7%)
  other arithmetic  15.4 us (5%)
  waiting for transfers between devices  10.4 us (3%)
    psum x2, blocking collectives, body(): first_grad = lax.psum(first_part, ('scen', 'blk')).reshape(-1)  157 us
    all_gather x1, blocking collectives, body(): lax.all_gather(first_section, 'scen', axis=0, tiled=True)  15.6 us
    dot_general x2, matrix products, body(): jnp.einsum('snc,nrc->snr', picked_cols, local_tiles, preferred_element_ty...  15.2 us
    dot_general x2, matrix products, body(): jnp.einsum('snr,nrc->snc', picked, local_tiles, preferred_element_type=jn...  12.1 us
    all_to_all x2, starting transfers between devices, body(): came = lax.all_to_all(sent, 'blk', split_axis=1, concat_axis=1, tiled=True)  11.6 us
    all_gather x1, blocking collectives, body(): lax.all_gather(first_cost, 'scen', axis=0, tiled=True)  10.1 us
    all_to_all x2, starting transfers between devices, body(): lax.all_to_all(partial_value, 'blk', split_axis=1, concat_axis=1, tiled=T...  9.88 us
    all_to_all x2, waiting for transfers between devices, body(): lax.all_to_all(partial_value, 'blk', split_axis=1, concat_axis=1, tiled=T...  9.01 us
  transfers between devices with their start and end apart: 5, of which 3 were waited for; matrix products, arithmetic and copies ran while one was open for 16% of the time, Pallas kernels for 0%

commit v1 on v0

v1 whole, which is shorter than its diff:
```python
import functools

import jax
import jax.numpy as jnp
from jax import lax
from jax.experimental import pallas as pl
from jax.experimental.pallas import tpu as pltpu
from jax.sharding import PartitionSpec as P

TILE = 128
ITERS = 2
S = 32
RB = 40
CB = 32
NL = 224
NF = 32
NK = 16
XB = 2
NS = 8
NB = 32
FB = XB * NS
W = 256
WF = 128
SPLIT = 128

PRIMAL = 0.4
FIRST = 2.0
DUAL = 0.4
LIMITS = (NL - 1, RB - 1, 1, NL, NL - 1, CB - 1, 1, NL)
FAR_LIMITS = (NF - 1, CB - 1, 1, NF)
MESH = pl.DeviceIdType.MESH
F32 = jnp.float32
BF16 = jnp.bfloat16


def dot(a, b):
    return jnp.dot(a, b, preferred_element_type=F32)


def dot_t(a, b):
    return lax.dot_general(a, b, (((1,), (1,)), ((), ())), preferred_element_type=F32)


def whole(value, top):
    return jnp.clip(value[0:1].astype(jnp.int32), 0, top)


def sorted_tables(key, other, count, width, empty):
    rows = lax.broadcasted_iota(jnp.int32, (width, width), 0).astype(F32)
    lanes = lax.broadcasted_iota(jnp.int32, (width, width), 1).astype(F32)
    key_j = jnp.broadcast_to(key[0:1], (width, width))
    key_i = key_j.T
    before = (key_j * W + lanes) < (key_i * W + rows)
    rank = dot(before.astype(F32).astype(BF16), jnp.ones((width, width), BF16))
    place = (rank == lanes).astype(F32).astype(BF16)
    lane8 = lax.broadcasted_iota(jnp.int32, (8, width), 1).astype(F32)
    source = jnp.concatenate([lane8, other, key, key], axis=0).astype(BF16)
    moved = dot(source, place)
    order, other_sorted, key_sorted = moved[0:8], moved[8:16], moved[16:24]
    previous = pltpu.roll(key_sorted, 1, 1)
    keep = ((key_sorted == previous) & (lane8 > 0)).astype(F32)
    ones = jnp.ones((16, width), BF16)
    upto = dot(ones, (key_i <= lanes).astype(F32).astype(BF16))[0:8]
    under = dot(ones, (key_i < lanes).astype(F32).astype(BF16))[0:8]
    last = jnp.where(upto > under, upto - 1.0, float(empty))
    return order, other_sorted, keep, last


def kernel(
    far_rows_s,
    far_cols_s,
    link_rows_s,
    link_cols_s,
    local_rows_v,
    local_cols_v,
    far_rows_v,
    cost_v,
    first_cost_v,
    first_v,
    local_hbm,
    far_hbm,
    link_hbm,
    inflow_hbm,
    rec_hbm,
    dual_hbm,
    first_out,
    rec_out,
    dual_out,
    tiles,
    far,
    link,
    inflow,
    half,
    hsum,
    bars,
    run,
    run_far,
    run_want,
    link_lhs,
    link_img,
    table_v,
    table_far_v,
    table_want_v,
    table,
    table_far,
    table_want,
    idx_send,
    idx_recv,
    term_send,
    term_recv,
    col_send,
    col_recv,
    z_send,
    z_recv,
    b_send,
    b_recv,
    bar_recv,
    load_sem,
    idx_sem,
    sems,
):
    me_s = lax.axis_index("scen")
    me_b = lax.axis_index("blk")
    mx, my, mc = me_b // 8, (me_b // 2) % 4, me_b % 2

    def peer(k):
        j = ((k + 1) * 13) % 32
        jx, jy, jc = j // 8, (j // 2) % 4, j % 2
        return (((mx + jx) % 4) * 4 + (my + jy) % 4) * 2 + (mc + jc) % 2

    def z_peer(k):
        return (me_s + k) % NS

    barrier = pltpu.get_barrier_semaphore()

    def greet(k, c):
        pl.semaphore_signal(barrier, inc=1, device_id=(me_s, peer(k)), device_id_type=MESH)
        return c

    lax.fori_loop(0, NB - 1, greet, 0)

    def greet_z(k, c):
        pl.semaphore_signal(barrier, inc=1, device_id=(z_peer(k), me_b), device_id_type=MESH)
        return c

    lax.fori_loop(1, NS, greet_z, 0)

    loads = [
        pltpu.make_async_copy(dual_hbm, dual_out, load_sem.at[0]),
        pltpu.make_async_copy(far_hbm, far, load_sem.at[1]),
        pltpu.make_async_copy(link_hbm, link, load_sem.at[2]),
        pltpu.make_async_copy(local_hbm, tiles, load_sem.at[3]),
        pltpu.make_async_copy(rec_hbm, rec_out, load_sem.at[4]),
        pltpu.make_async_copy(inflow_hbm, inflow, load_sem.at[5]),
    ]
    for load in loads:
        load.start()

    for p in range(NB):
        idx_send[p] = jnp.full((8, TILE), far_cols_s[p], jnp.int32)

    pad = jnp.full((8, W - NL), 64.0, F32)
    row_key = jnp.concatenate(
        [jnp.broadcast_to(local_rows_v[...].astype(F32), (8, NL)), pad], axis=1
    )
    col_key = jnp.concatenate(
        [jnp.broadcast_to(local_cols_v[...].astype(F32), (8, NL)), pad], axis=1
    )
    pad_far = jnp.full((8, WF - NF), 64.0, F32)
    far_key = jnp.concatenate(
        [jnp.broadcast_to(far_rows_v[...].astype(F32), (8, NF)), pad_far], axis=1
    )
    col_tables = sorted_tables(col_key, row_key, NL, W, NL)
    row_tables = sorted_tables(row_key, col_key, NL, W, NL)
    for i, value in enumerate(col_tables + row_tables):
        table_v[i : i + 1, :] = whole(value, LIMITS[i])
    far_tables = sorted_tables(far_key, far_key, NF, WF, NF)
    for i, value in enumerate(far_tables):
        table_far_v[i : i + 1, :] = whole(value, FAR_LIMITS[i])
    to_smem = [
        pltpu.make_async_copy(table_v, table, load_sem.at[6]),
        pltpu.make_async_copy(table_far_v, table_far, load_sem.at[7]),
    ]
    for copy in to_smem:
        copy.start()
    zero = jnp.zeros((S, TILE), F32)
    run[NL] = zero
    run_far[NF] = zero
    run_want[NF] = zero

    loads[0].wait()

    def to_half(rb, c):
        value = dual_out[:, pl.ds(pl.multiple_of(rb * TILE, TILE), TILE)].astype(BF16)
        half[rb] = value
        hsum[pl.ds(rb, 1), :] = jnp.sum(value.astype(F32), axis=0, keepdims=True)
        return c

    lax.fori_loop(0, RB, to_half, 0, unroll=8)
    loads[1].wait()

    for it in range(ITERS):
        def send_index(k, c):
            p = peer(k)
            pltpu.make_async_remote_copy(
                src_ref=idx_send.at[p],
                dst_ref=idx_recv.at[me_b],
                send_sem=idx_sem.at[0],
                recv_sem=idx_sem.at[1],
                device_id=(me_s, p),
                device_id_type=MESH,
            ).start()
            return c

        def far_term(k, c):
            p = peer(k)
            term_send[it, p] = dot(half[far_rows_s[p]], far[p]).astype(BF16)
            return c

        def send_term(k, c):
            p = peer(k)
            pltpu.make_async_remote_copy(
                src_ref=term_send.at[it, p],
                dst_ref=term_recv.at[it, me_b],
                send_sem=sems.at[it, 0, 0],
                recv_sem=sems.at[it, 0, 1],
                device_id=(me_s, p),
                device_id_type=MESH,
            ).start()
            return c

        for g in range(0, NB, 16):
            lax.fori_loop(g, g + 16, far_term, 0, unroll=16)
            if it == 0 and g == 0:
                pl.semaphore_wait(barrier, NB - 1 + NS - 1)
            lax.fori_loop(g, min(g + 16, NB - 1), send_term, 0)
        if it == 0:
            lax.fori_loop(0, NB - 1, send_index, 0)
        term_recv[it, me_b] = term_send[it, me_b]

        if it == 0:
            loads[2].wait()
        for n in range(NK):
            link_lhs[n : n + 1, :] = hsum[pl.ds(link_rows_s[n], 1), :]
        sums = link_lhs[...]
        high = sums.astype(BF16)
        low = (sums - high.astype(F32)).astype(BF16)
        lhs = jnp.concatenate([high, low], axis=0)
        block = lax.broadcasted_iota(jnp.int32, (FB, TILE), 0)
        part = jnp.zeros((FB, TILE), F32)
        for n in range(NK):
            product = dot(lhs, link[n])
            row = product[n : n + 1] + product[NK + n : NK + n + 1]
            part = part + jnp.where(block == link_cols_s[n], row, 0.0)
        for g in range(NS):
            z_send[it, g] = part[g * XB : (g + 1) * XB]

        def send_z(k, c):
            s = z_peer(k)
            pltpu.make_async_remote_copy(
                src_ref=z_send.at[it, s],
                dst_ref=z_recv.at[it, me_s],
                send_sem=sems.at[it, 1, 0],
                recv_sem=sems.at[it, 1, 1],
                device_id=(s, me_b),
                device_id_type=MESH,
            ).start()
            return c

        lax.fori_loop(1, NS, send_z, 0)
        z_recv[it, me_s] = z_send[it, me_s]

        if it == 0:
            for copy in to_smem:
                copy.wait()
            loads[3].wait()

        def gradient_step(n, total):
            keep = table[2, n].astype(F32)
            total = total * keep + dot(half[table[1, n]], tiles[table[0, n]])
            run[n] = total
            return total

        total = lax.fori_loop(0, SPLIT, gradient_step, zero, unroll=32)

        pltpu.make_async_copy(
            z_recv.at[it, pl.ds(0, NS - 1)], z_recv.at[it, pl.ds(0, NS - 1)], sems.at[it, 1, 1]
        ).wait()
        b_send[it] = jnp.sum(z_recv[it], axis=0)

        def send_b(k, c):
            pltpu.make_async_remote_copy(
                src_ref=b_send.at[it],
                dst_ref=b_recv.at[it, me_b],
                send_sem=sems.at[it, 2, 0],
                recv_sem=sems.at[it, 2, 1],
                device_id=(me_s, peer(k)),
                device_id_type=MESH,
            ).start()
            return c

        lax.fori_loop(0, NB - 1, send_b, 0)
        b_recv[it, me_b] = b_send[it]
        lax.fori_loop(SPLIT, NL, gradient_step, total, unroll=32)

        if it == 0:
            pltpu.make_async_copy(
                idx_recv.at[pl.ds(0, NB - 1)], idx_recv.at[pl.ds(0, NB - 1)], idx_sem.at[1]
            ).wait()
            idx_recv[me_b] = idx_send[me_b]
            lane = lax.broadcasted_iota(jnp.int32, (8, WF), 1)
            wanted = jnp.full((8, WF), 64, jnp.int32)
            for q in range(NB):
                wanted = jnp.where(lane == q, idx_recv[q], wanted)
            wanted = wanted.astype(F32)
            want_tables = sorted_tables(wanted, wanted, NF, WF, NF)
            for i, value in enumerate((want_tables[0], wanted) + want_tables[2:]):
                table_want_v[i : i + 1, :] = whole(value, FAR_LIMITS[i])
            want_copy = pltpu.make_async_copy(table_want_v, table_want, load_sem.at[6])
            want_copy.start()
            want_copy.wait()
            loads[4].wait()

        pltpu.make_async_copy(
            term_recv.at[it, pl.ds(0, NB - 1)],
            term_recv.at[it, pl.ds(0, NB - 1)],
            sems.at[it, 0, 1],
        ).wait()

        def want_step(k, total):
            keep = table_want[2, k].astype(F32)
            total = total * keep + term_recv[it, table_want[0, k]].astype(F32)
            run_want[k] = total
            return total

        lax.fori_loop(0, NF, want_step, zero, unroll=8)

        def update_recourse(cb, c):
            at = pl.ds(pl.multiple_of(cb * TILE, TILE), TILE)
            grad = run[table[3, cb]] + run_want[table_want[3, cb]]
            old = rec_out[:, at]
            new = jnp.maximum(old - PRIMAL * (cost_v[:, at] - grad), 0.0)
            bars[cb] = (2.0 * new - old).astype(BF16)
            rec_out[:, at] = new
            return c

        lax.fori_loop(0, CB, update_recourse, 0, unroll=8)

        def gather_col(k, c):
            p = peer(k)
            col_send[it, p] = bars[table_want[1, p]]
            return c

        def send_col(k, c):
            p = peer(k)
            pltpu.make_async_remote_copy(
                src_ref=col_send.at[it, p],
                dst_ref=col_recv.at[it, me_b],
                send_sem=sems.at[it, 3, 0],
                recv_sem=sems.at[it, 3, 1],
                device_id=(me_s, p),
                device_id_type=MESH,
            ).start()
            return c

        lax.fori_loop(0, NB, gather_col, 0, unroll=8)
        lax.fori_loop(0, NB - 1, send_col, 0)
        col_recv[it, me_b] = col_send[it, me_b]

        pltpu.make_async_copy(
            b_recv.at[it, pl.ds(0, NB - 1)], b_recv.at[it, pl.ds(0, NB - 1)], sems.at[it, 2, 1]
        ).wait()
        first_grad = jnp.sum(b_recv[it], axis=0)
        old_first = first_v[...] if it == 0 else first_out[...]
        new_first = jnp.maximum(
            old_first - FIRST * (first_cost_v[...] - first_grad / (S * NS)), 0.0
        )
        first_out[...] = new_first
        bar_recv[it, me_s] = (2.0 * new_first - old_first).astype(BF16).astype(F32)

        def send_bar(k, c):
            pltpu.make_async_remote_copy(
                src_ref=bar_recv.at[it, me_s],
                dst_ref=bar_recv.at[it, me_s],
                send_sem=sems.at[it, 4, 0],
                recv_sem=sems.at[it, 4, 1],
                device_id=(z_peer(k), me_b),
                device_id_type=MESH,
            ).start()
            return c

        lax.fori_loop(1, NS, send_bar, 0)

        def image_step(n, total):
            keep = table[6, n].astype(F32)
            total = total * keep + dot_t(bars[table[5, n]], tiles[table[4, n]])
            run[n] = total
            return total

        lax.fori_loop(0, NL, image_step, zero, unroll=32)

        pltpu.make_async_copy(
            bar_recv.at[it, pl.ds(0, NS - 1)], bar_recv.at[it, pl.ds(0, NS - 1)], sems.at[it, 4, 1]
        ).wait()
        for n in range(NK):
            b = link_cols_s[n]
            link_lhs[n : n + 1, :] = bar_recv[it, b // XB, pl.ds(b % XB, 1), :]
        lhs = link_lhs[...].astype(BF16)
        block = lax.broadcasted_iota(jnp.int32, (RB, TILE), 0)
        image = jnp.zeros((RB, TILE), F32)
        for n in range(NK):
            row = dot_t(lhs, link[n])[n : n + 1]
            image = image + jnp.where(block == link_rows_s[n], row, 0.0)
        link_img[...] = image

        pltpu.make_async_copy(
            col_recv.at[it, pl.ds(0, NB - 1)],
            col_recv.at[it, pl.ds(0, NB - 1)],
            sems.at[it, 3, 1],
        ).wait()

        def far_step(k, total):
            q = table_far[0, k]
            keep = table_far[2, k].astype(F32)
            total = total * keep + dot_t(col_recv[it, q], far[q])
            run_far[k] = total
            return total

        lax.fori_loop(0, NF, far_step, zero, unroll=32)
        if it == 0:
            loads[5].wait()

        def update_duals(rb, c):
            at = pl.ds(pl.multiple_of(rb * TILE, TILE), TILE)
            image = run[table[7, rb]] + run_far[table_far[3, rb]] + link_img[pl.ds(rb, 1), :]
            new = dual_out[:, at] + DUAL * (inflow[:, at].astype(F32) - image)
            dual_out[:, at] = new
            if it < ITERS - 1:
                value = new.astype(BF16)
                half[rb] = value
                hsum[pl.ds(rb, 1), :] = jnp.sum(value.astype(F32), axis=0, keepdims=True)
            return c

        lax.fori_loop(0, RB, update_duals, 0, unroll=8)

    def sent(buffer, sem):
        pltpu.make_async_copy(buffer, buffer, sem).wait()

    sent(idx_recv.at[pl.ds(0, NB - 1)], idx_sem.at[0])
    for it in range(ITERS):
        sent(term_recv.at[it, pl.ds(0, NB - 1)], sems.at[it, 0, 0])
        sent(z_recv.at[it, pl.ds(0, NS - 1)], sems.at[it, 1, 0])
        sent(b_recv.at[it, pl.ds(0, NB - 1)], sems.at[it, 2, 0])
        sent(col_recv.at[it, pl.ds(0, NB - 1)], sems.at[it, 3, 0])
        sent(bar_recv.at[it, pl.ds(0, NS - 1)], sems.at[it, 4, 0])


def body(
    local_tiles,
    local_rows,
    local_cols,
    far_tiles,
    far_rows,
    far_cols,
    link_tiles,
    link_rows,
    link_cols,
    inflows,
    recourse_cost,
    first_cost,
    first_section,
    recourse,
    duals,
):
    smem = pl.BlockSpec(memory_space=pltpu.SMEM)
    vmem = pl.BlockSpec(memory_space=pltpu.VMEM)
    hbm = pl.BlockSpec(memory_space=pl.ANY)
    dma = pltpu.SemaphoreType.DMA
    first_out, rec_out, dual_out = pl.pallas_call(
        kernel,
        out_shape=(
            jax.ShapeDtypeStruct((XB, TILE), F32),
            jax.ShapeDtypeStruct((S, CB * TILE), F32),
            jax.ShapeDtypeStruct((S, RB * TILE), F32),
        ),
        in_specs=[smem] * 4 + [vmem] * 6 + [hbm] * 6,
        out_specs=(vmem, vmem, vmem),
        scratch_shapes=[
            pltpu.VMEM((NL, TILE, TILE), BF16),
            pltpu.VMEM((NF, TILE, TILE), BF16),
            pltpu.VMEM((NK, TILE, TILE), BF16),
            pltpu.VMEM((S, RB * TILE), BF16),
            pltpu.VMEM((RB, S, TILE), BF16),
            pltpu.VMEM((RB, TILE), F32),
            pltpu.VMEM((CB, S, TILE), BF16),
            pltpu.VMEM((NL + 1, S, TILE), F32),
            pltpu.VMEM((NF + 1, S, TILE), F32),
            pltpu.VMEM((NF + 1, S, TILE), F32),
            pltpu.VMEM((NK, TILE), F32),
            pltpu.VMEM((RB, TILE), F32),
            pltpu.VMEM((8, W), jnp.int32),
            pltpu.VMEM((4, WF), jnp.int32),
            pltpu.VMEM((4, WF), jnp.int32),
            pltpu.SMEM((8, W), jnp.int32),
            pltpu.SMEM((4, WF), jnp.int32),
            pltpu.SMEM((4, WF), jnp.int32),
            pltpu.VMEM((NB, 8, TILE), jnp.int32),
            pltpu.VMEM((NB, 8, TILE), jnp.int32),
            pltpu.VMEM((ITERS, NB, S, TILE), BF16),
            pltpu.VMEM((ITERS, NB, S, TILE), BF16),
            pltpu.VMEM((ITERS, NB, S, TILE), BF16),
            pltpu.VMEM((ITERS, NB, S, TILE), BF16),
            pltpu.VMEM((ITERS, NS, XB, TILE), F32),
            pltpu.VMEM((ITERS, NS, XB, TILE), F32),
            pltpu.VMEM((ITERS, XB, TILE), F32),
            pltpu.VMEM((ITERS, NB, XB, TILE), F32),
            pltpu.VMEM((ITERS, NS, XB, TILE), F32),
            dma((8,)),
            dma((2,)),
            dma((ITERS, 5, 2)),
        ],
        compiler_params=pltpu.CompilerParams(
            collective_id=0, has_side_effects=True, vmem_limit_bytes=48 << 20
        ),
        name="dispatch",
    )(
        far_rows.reshape(NF),
        far_cols.reshape(NF),
        link_rows,
        link_cols,
        local_rows.reshape(1, NL),
        local_cols.reshape(1, NL),
        far_rows.reshape(1, NF),
        recourse_cost.reshape(1, CB * TILE),
        first_cost.reshape(XB, TILE),
        first_section.reshape(XB, TILE),
        local_tiles,
        far_tiles.reshape(NF, TILE, TILE),
        link_tiles,
        inflows,
        recourse,
        duals,
    )
    return first_out.reshape(XB * TILE), rec_out, dual_out


def solution(mesh):
    in_specs = (
        P("blk", None, None),
        P("blk"),
        P("blk"),
        P("blk", None, None, None),
        P("blk", None),
        P("blk", None),
        P(("scen", "blk"), None, None),
        P(("scen", "blk")),
        P(("scen", "blk")),
        P("scen", "blk"),
        P("blk"),
        P("scen"),
        P("scen"),
        P("scen", "blk"),
        P("scen", "blk"),
    )
    out_specs = (P("scen"), P("scen", "blk"), P("scen", "blk"))
    return jax.shard_map(body, mesh=mesh, in_specs=in_specs, out_specs=out_specs, check_vma=False)
```

time: 306 us -> 64.2 us (0.21)
  blocking collectives: 183 us -> 0 us
  Pallas kernels: 0 us -> 49.4 us
  matrix products: 44.1 us -> 0 us
  starting transfers between devices: 30 us -> 0 us
  other arithmetic: 15.4 us -> 0 us
  waiting for transfers between devices: 10.4 us -> 0 us
  local copies, waits for them, and re-layouts: 20.6 us -> 13.6 us
    psum x2 -> x0, blocking collectives: 157 us -> none  [body(): first_grad = lax.psum(first_part, ('scen', 'blk')).reshape(-1)]
    pallas_call x0 -> x1, Pallas kernels: none -> 49.4 us  [body(): pl.pallas_call(kernel, out_shape=(jax.ShapeDtypeStruct((XB, TILE), F32),...]
    dot_general x24 -> x0, matrix products: 44.1 us -> none  [the longest x2 15.2 us: body(): jnp.einsum('snc,nrc->snr', picked_cols, local_tiles, preferred_element_ty...]
    all_to_all x5 -> x0, starting transfers between devices: 30 us -> none  [the longest x2 11.6 us: body(): came = lax.all_to_all(sent, 'blk', split_axis=1, concat_axis=1, tiled=True)]
    all_gather x2 -> x0, blocking collectives: 25.7 us -> none  [the longest x1 15.6 us: body(): lax.all_gather(first_section, 'scen', axis=0, tiled=True)]
    gather x12 -> x0, local copies, waits for them, and re-layouts: 14.7 us -> none  [the longest x2 4.4 us: body(): picked_cols = jnp.take(extrapolated, local_cols, axis=1)]
    all_to_all x5 -> x0, waiting for transfers between devices: 10.4 us -> none  [the longest x2 9.01 us: body(): lax.all_to_all(partial_value, 'blk', split_axis=1, concat_axis=1, tiled=T...]
    unnamed x86 -> x31, local copies, waits for them, and re-layouts: 3.78 us -> 13.6 us
  transfers between devices with their start and end apart: 5 -> 0, of which waited for: 3 -> 0; matrix products, arithmetic and copies ran while one was open for 16% -> 0% of each run, Pallas kernels for 0% -> 0%
where the time goes in v1:
time: 64.2 us; the launch traced here: 63.7 us
  Pallas kernels  49.4 us (77%)
  local copies, waits for them, and re-layouts  13.6 us (21%)
  between operations  0.67 us (1%)
    pallas_call x1, Pallas kernels, body(): pl.pallas_call(kernel, out_shape=(jax.ShapeDtypeStruct((XB, TILE), F32),...  49.4 us
    unnamed x31, local copies, waits for them, and re-layouts  13.6 us

profile of v1, /device:TPU:1, one launch (start us, length us, event | category | flops | bytes accessed | tf_op | source)
XLA Modules:
  0.0 63.7 jit_solution(12400318777533736701)
XLA Ops:
  0.6 0.0 copy-start
  0.6 1.2 %copy-done = bf16[32,1,128,128]{3,2,1,0:T(8,128)(2,1)S(1)} copy-done((bf16[32,1,128,128]{3,2,1,0:T(8,128)(2,1)S(1)}, bf16[32,1,128,128]{3,2,1,0:T(8,128)(2,1)}, u32[]{:S(2)}) %copy-start) | copy-done | bytes 1048600
  1.9 0.0 copy-start.1
  1.9 1.1 %copy-done.1 = f32[32,5120]{1,0:T(8,128)S(1)} copy-done((f32[32,5120]{1,0:T(8,128)S(1)}, f32[32,5120]{1,0:T(8,128)}, u32[]{:S(2)}) %copy-start.1) | copy-done | bytes 655384
  3.0 0.0 copy-start.2
  3.0 1.0 %copy-done.2 = bf16[16,128,128]{2,1,0:T(8,128)(2,1)S(1)} copy-done((bf16[16,128,128]{2,1,0:T(8,128)(2,1)S(1)}, bf16[16,128,128]{2,1,0:T(8,128)(2,1)}, u32[]{:S(2)}) %copy-start.2) | copy-done | bytes 524312
  4.0 0.0 copy-start.3
  4.0 1.0 %copy-done.3 = f32[32,4096]{1,0:T(8,128)S(1)} copy-done((f32[32,4096]{1,0:T(8,128)S(1)}, f32[32,4096]{1,0:T(8,128)}, u32[]{:S(2)}) %copy-start.3) | copy-done | bytes 524312
  5.0 0.0 copy-start.4
  5.0 1.0 %copy-done.4 = bf16[32,5120]{1,0:T(8,128)(2,1)S(1)} copy-done((bf16[32,5120]{1,0:T(8,128)(2,1)S(1)}, bf16[32,5120]{1,0:T(8,128)(2,1)}, u32[]{:S(2)}) %copy-start.4) | copy-done | bytes 327704
  6.0 0.0 copy-start.5
  6.0 0.7 %copy-done.5 = f32[4096]{0:T(1024)S(1)} copy-done((f32[4096]{0:T(1024)S(1)}, f32[4096]{0:T(1024)}, u32[]{:S(2)}) %copy-start.5) | copy-done | bytes 16408
  6.7 0.0 copy-start.6
  6.7 0.7 %copy-done.6 = s32[32,1]{0,1:T(1,128)S(1)} copy-done((s32[32,1]{0,1:T(1,128)S(1)}, s32[32,1]{0,1:T(1,128)}, u32[]{:S(2)}) %copy-start.6) | copy-done | bytes 152
  7.4 0.0 copy-start.7
  7.4 0.7 %copy-done.7 = s32[224]{0:T(256)S(1)} copy-done((s32[224]{0:T(256)S(1)}, s32[224]{0:T(256)}, u32[]{:S(2)}) %copy-start.7) | copy-done | bytes 920
  8.1 0.0 copy-start.8
  8.1 0.7 %copy-done.8 = s32[224]{0:T(256)S(1)} copy-done((s32[224]{0:T(256)S(1)}, s32[224]{0:T(256)}, u32[]{:S(2)}) %copy-start.8) | copy-done | bytes 920
  8.7 0.0 copy-start.9
  8.7 0.7 %copy-done.9 = f32[256]{0:T(256)S(1)} copy-done((f32[256]{0:T(256)S(1)}, f32[256]{0:T(256)}, u32[]{:S(2)}) %copy-start.9) | copy-done | bytes 1048
  9.4 0.0 copy-start.10
  9.4 0.7 %copy-done.10 = f32[256]{0:T(256)S(1)} copy-done((f32[256]{0:T(256)S(1)}, f32[256]{0:T(256)}, u32[]{:S(2)}) %copy-start.10) | copy-done | bytes 1048
  10.1 0.0 copy-start.11
  10.1 0.7 %copy-done.11 = s32[32,1]{0,1:T(1,128)S(1)} copy-done((s32[32,1]{0,1:T(1,128)S(1)}, s32[32,1]{0,1:T(1,128)}, u32[]{:S(2)}) %copy-start.11) | copy-done | bytes 152
  10.8 0.0 copy-start.12
  10.8 0.7 %copy-done.12 = s32[16]{0:T(128)S(1)} copy-done((s32[16]{0:T(128)S(1)}, s32[16]{0:T(128)}, u32[]{:S(2)}) %copy-start.12) | copy-done | bytes 88
  11.4 0.0 copy-start.13
  11.4 0.7 %copy-done.13 = s32[16]{0:T(128)S(1)} copy-done((s32[16]{0:T(128)S(1)}, s32[16]{0:T(128)}, u32[]{:S(2)}) %copy-start.13) | copy-done | bytes 88
  12.1 49.4 %dispatch.1 = (f32[2,128]{1,0:T(2,128)S(1)}, f32[32,4096]{1,0:T(8,128)S(1)}, f32[32,5120]{1,0:T(8,128)S(1)}) custom-call(s32[32]{0:T(128)S(1)} %bitcast.12, s32[32]{0:T(128)S(1)} %bitcast.19, s32[16]{0:T(128)S(1)} %copy-done.12, s32[16]{0:T(128)S(1)} %copy-done.13, s32[1,224]{1,0:T(1,128)S(1)} %bitcast.15, s32[1,224]{1,0:T(1,128)S(1)} %bitcast.16, ...), custom_call_target="tpu_custom_call" | custom-call | tf_op jit(solution)/shard_map/dispatch/pallas_call | solution.py:479
  61.5 0.6 copy.21
  62.1 0.8 %copy.22 = f32[32,4096]{1,0:T(8,128)} copy(f32[32,4096]{1,0:T(8,128)S(1)} %get-tuple-element.13) | data formatting | bytes 1048576
  62.9 0.8 %copy.23 = f32[32,5120]{1,0:T(8,128)} copy(f32[32,5120]{1,0:T(8,128)S(1)} %get-tuple-element.14) | data formatting | bytes 1310720
Async XLA Ops:
  0.6 1.2 %copy-start = (bf16[32,1,128,128]{3,2,1,0:T(8,128)(2,1)S(1)}, bf16[32,1,128,128]{3,2,1,0:T(8,128)(2,1)}, u32[]{:S(2)}) copy-start(bf16[32,1,128,128]{3,2,1,0:T(8,128)(2,1)} %param.18) | copy-start | bytes 3145732
  1.9 1.1 %copy-start.1 = (f32[32,5120]{1,0:T(8,128)S(1)}, f32[32,5120]{1,0:T(8,128)}, u32[]{:S(2)}) copy-start(f32[32,5120]{1,0:T(8,128)} %dual_hbm.1) | copy-start | bytes 1966084
  3.0 1.0 %copy-start.2 = (bf16[16,128,128]{2,1,0:T(8,128)(2,1)S(1)}, bf16[16,128,128]{2,1,0:T(8,128)(2,1)}, u32[]{:S(2)}) copy-start(bf16[16,128,128]{2,1,0:T(8,128)(2,1)} %link_hbm.1) | copy-start | bytes 1572868
  4.0 1.0 %copy-start.3 = (f32[32,4096]{1,0:T(8,128)S(1)}, f32[32,4096]{1,0:T(8,128)}, u32[]{:S(2)}) copy-start(f32[32,4096]{1,0:T(8,128)} %rec_hbm.1) | copy-start | bytes 1572868
  5.0 1.0 %copy-start.4 = (bf16[32,5120]{1,0:T(8,128)(2,1)S(1)}, bf16[32,5120]{1,0:T(8,128)(2,1)}, u32[]{:S(2)}) copy-start(bf16[32,5120]{1,0:T(8,128)(2,1)} %inflow_hbm.1) | copy-start | bytes 983044
  6.0 0.7 %copy-start.5 = (f32[4096]{0:T(1024)S(1)}, f32[4096]{0:T(1024)}, u32[]{:S(2)}) copy-start(f32[4096]{0:T(1024)} %param.25) | copy-start | bytes 49156
  6.7 0.7 %copy-start.6 = (s32[32,1]{0,1:T(1,128)S(1)}, s32[32,1]{0,1:T(1,128)}, u32[]{:S(2)}) copy-start(s32[32,1]{0,1:T(1,128)} %param.19) | copy-start | bytes 388
  7.4 0.7 %copy-start.7 = (s32[224]{0:T(256)S(1)}, s32[224]{0:T(256)}, u32[]{:S(2)}) copy-start(s32[224]{0:T(256)} %param.16) | copy-start | bytes 2692
  8.1 0.7 %copy-start.8 = (s32[224]{0:T(256)S(1)}, s32[224]{0:T(256)}, u32[]{:S(2)}) copy-start(s32[224]{0:T(256)} %param.17) | copy-start | bytes 2692
  8.7 0.7 %copy-start.9 = (f32[256]{0:T(256)S(1)}, f32[256]{0:T(256)}, u32[]{:S(2)}) copy-start(f32[256]{0:T(256)} %param.26) | copy-start | bytes 3076
  9.4 0.7 %copy-start.10 = (f32[256]{0:T(256)S(1)}, f32[256]{0:T(256)}, u32[]{:S(2)}) copy-start(f32[256]{0:T(256)} %param.27) | copy-start | bytes 3076
  10.1 0.7 %copy-start.11 = (s32[32,1]{0,1:T(1,128)S(1)}, s32[32,1]{0,1:T(1,128)}, u32[]{:S(2)}) copy-start(s32[32,1]{0,1:T(1,128)} %param.20) | copy-start | bytes 388
  10.8 0.7 %copy-start.12 = (s32[16]{0:T(128)S(1)}, s32[16]{0:T(128)}, u32[]{:S(2)}) copy-start(s32[16]{0:T(128)} %link_rows_s.1) | copy-start | bytes 196
  11.4 0.7 %copy-start.13 = (s32[16]{0:T(128)S(1)}, s32[16]{0:T(128)}, u32[]{:S(2)}) copy-start(s32[16]{0:T(128)} %link_cols_s.1) | copy-start | bytes 196

commit v2 on v1

v2 whole, which is shorter than its diff:
```python
import functools

import jax
import jax.numpy as jnp
from jax import lax
from jax.experimental import pallas as pl
from jax.experimental.pallas import tpu as pltpu
from jax.sharding import PartitionSpec as P

TILE = 128
ITERS = 2
S = 32
RB = 40
CB = 32
NL = 224
NF = 32
NK = 16
XB = 2
NS = 8
NB = 32
FB = XB * NS
W = 256
WF = 128
STEPS = sorted(
    ((a, b) for a in range(4) for b in range(4)),
    key=lambda d: -(min(d[0], 4 - d[0]) + min(d[1], 4 - d[1])),
)
ORDER = [(a, b, c) for c in (1, 0) for a, b in STEPS]
GROUPS = tuple(
    tuple(i for i in range(NB - 1) if i % 16 in part)
    for part in (range(0, 5), range(5, 11), range(11, 16))
)
UNROLL = 56

PRIMAL = 0.4
FIRST = 2.0
DUAL = 0.4
LIMITS = (NL - 1, RB - 1, 1, NL, NL - 1, CB - 1, 1, NL)
FAR_LIMITS = (NF - 1, CB - 1, 1, NF)
MESH = pl.DeviceIdType.MESH
F32 = jnp.float32
BF16 = jnp.bfloat16


def dot(a, b):
    return jnp.dot(a, b, preferred_element_type=F32)


def dot_t(a, b):
    return lax.dot_general(a, b, (((1,), (1,)), ((), ())), preferred_element_type=F32)


def whole(value, top):
    return jnp.clip(value[0:1].astype(jnp.int32), 0, top)


def sorted_tables(key, other, count, width, empty):
    rows = lax.broadcasted_iota(jnp.int32, (width, width), 0).astype(F32)
    lanes = lax.broadcasted_iota(jnp.int32, (width, width), 1).astype(F32)
    key_j = jnp.broadcast_to(key[0:1], (width, width))
    key_i = key_j.T
    before = (key_j * W + lanes) < (key_i * W + rows)
    rank = dot(before.astype(F32).astype(BF16), jnp.ones((width, width), BF16))
    place = (rank == lanes).astype(F32).astype(BF16)
    lane8 = lax.broadcasted_iota(jnp.int32, (8, width), 1).astype(F32)
    source = jnp.concatenate([lane8, other, key, key], axis=0).astype(BF16)
    moved = dot(source, place)
    order, other_sorted, key_sorted = moved[0:8], moved[8:16], moved[16:24]
    previous = pltpu.roll(key_sorted, 1, 1)
    keep = ((key_sorted == previous) & (lane8 > 0)).astype(F32)
    ones = jnp.ones((16, width), BF16)
    under = dot(ones, (key_i < lanes).astype(F32).astype(BF16))[0:8]
    upto = pltpu.roll(under, width - 1, 1)
    last = jnp.where(upto > under, upto - 1.0, float(empty))
    return order, other_sorted, keep, last


def kernel(
    far_rows_h,
    far_cols_h,
    link_rows_h,
    link_cols_h,
    local_rows_h,
    local_cols_h,
    cost_h,
    first_cost_h,
    first_h,
    local_h,
    far_h,
    link_h,
    inflow_h,
    rec_h,
    dual_h,
    first_out,
    rec_out,
    dual_out,
    far_rows_s,
    far_cols_s,
    link_rows_s,
    link_cols_s,
    local_rows_v,
    local_cols_v,
    far_rows_v,
    cost_v,
    first_own,
    first_own_cost,
    first_recv,
    first_full,
    first_cost,
    tiles,
    far,
    far_t,
    link,
    inflow,
    rec,
    rec_base,
    rec_old,
    dual,
    dual_base,
    half,
    bars,
    run,
    run_far,
    run_want,
    product,
    link_lhs,
    link_img,
    table_v,
    table_far_v,
    table_want_v,
    table,
    table_far,
    table_want,
    idx_send,
    idx_recv,
    term_send,
    term_recv,
    col_send,
    col_recv,
    z_recv,
    b_recv,
    load_sem,
    out_sem,
    idx_sem,
    sems,
):
    me_s = lax.axis_index("scen")
    me_b = lax.axis_index("blk")
    mx, my, mc = me_b // 8, (me_b // 2) % 4, me_b % 2

    def peer(step):
        jx, jy, jc = step
        return (((mx + jx) % 4) * 4 + (my + jy) % 4) * 2 + (mc + jc) % 2

    def source(step):
        return peer(tuple(-d for d in step))

    def group_peer(k):
        return (me_s + k // 2) % NS, me_b - mc + (mc + k) % 2

    barrier = pltpu.get_barrier_semaphore()

    def greet(step):
        pl.semaphore_signal(barrier, inc=1, device_id=(me_s, peer(step)), device_id_type=MESH)

    for step in ORDER[:-1]:
        greet(step)

    def greet_z(k, c):
        z, b = group_peer(k)
        pl.semaphore_signal(barrier, inc=1, device_id=(z, b), device_id_type=MESH)
        return c

    lax.fori_loop(2, 2 * NS, greet_z, 0)

    def load(src, dst, i):
        copy = pltpu.make_async_copy(src, dst, load_sem.at[i])
        copy.start()
        return copy

    load_rows = load(local_rows_h, local_rows_v, 0)
    load_cols = load(local_cols_h, local_cols_v, 1)
    load_far_rows_v = load(far_rows_h, far_rows_v, 2)
    load_far_rows = load(far_rows_h, far_rows_s, 3)
    load_far_cols = load(far_cols_h, far_cols_s, 4)
    load_dual = load(dual_h, dual, 5)
    load_far = load(far_h, far, 6)
    load_link_rows = load(link_rows_h, link_rows_s, 7)
    load_link_cols = load(link_cols_h, link_cols_s, 8)
    load_link = load(link_h, link, 9)
    load_first = load(first_h, first_own, 10)
    load_first_cost = load(first_cost_h, first_own_cost, 11)
    load_tiles = load(local_h, tiles, 12)
    load_cost = load(cost_h, cost_v, 13)
    load_rec = load(rec_h, rec, 14)
    load_inflow = load(inflow_h, inflow, 15)

    load_rows.wait()
    load_cols.wait()
    load_far_rows_v.wait()
    pad = jnp.full((8, W - NL), 64.0, F32)
    row_key = jnp.concatenate(
        [jnp.broadcast_to(local_rows_v[...].astype(F32), (8, NL)), pad], axis=1
    )
    col_key = jnp.concatenate(
        [jnp.broadcast_to(local_cols_v[...].astype(F32), (8, NL)), pad], axis=1
    )
    pad_far = jnp.full((8, WF - NF), 64.0, F32)
    far_key = jnp.concatenate(
        [jnp.broadcast_to(far_rows_v[...].astype(F32), (8, NF)), pad_far], axis=1
    )
    col_tables = sorted_tables(col_key, row_key, NL, W, NL)
    row_tables = sorted_tables(row_key, col_key, NL, W, NL)
    for i, value in enumerate(col_tables + row_tables):
        table_v[i : i + 1, :] = whole(value, LIMITS[i])
    far_tables = sorted_tables(far_key, far_key, NF, WF, NF)
    for i, value in enumerate(far_tables):
        table_far_v[i : i + 1, :] = whole(value, FAR_LIMITS[i])
    to_smem = [load(table_v, table, 0), load(table_far_v, table_far, 1)]
    zero = jnp.zeros((S, TILE), F32)
    run[NL] = zero
    run_far[NF] = zero
    run_want[NF] = zero

    load_dual.wait()

    def first_half(rb, c):
        half[rb] = dual[:, pl.ds(pl.multiple_of(rb * TILE, TILE), TILE)].astype(BF16)
        return c

    lax.fori_loop(0, RB, first_half, 0, unroll=8)
    load_far_rows.wait()
    load_far.wait()

    def send_all(it, src, dst, which):
        def one(i):
            p = peer(ORDER[i])
            group = [i in g for g in GROUPS].index(True)
            pltpu.make_async_remote_copy(
                src_ref=src.at[it, p],
                dst_ref=dst.at[it, me_b],
                send_sem=sems.at[it, which, 3],
                recv_sem=sems.at[it, which, group],
                device_id=(me_s, p),
                device_id_type=MESH,
            ).start()

        return one

    def bytes_of(buffer, count, sem):
        view = buffer.at[pl.ds(0, count)]
        pltpu.make_async_copy(view, view, sem).wait()

    def new_duals(r, last):
        return dual_base[r] - DUAL * (run_far[last] + link_img[pl.ds(r, 1), :])

    def new_recourse(b, last):
        new = jnp.maximum(rec_base[b] + PRIMAL * run_want[last], 0.0)
        return new, (2.0 * new - rec_old[b]).astype(BF16)

    for it in range(ITERS):
        send_term = send_all(it, term_send, term_recv, 0)
        for g in range(0, NB, 8):
            for step in ORDER[g : g + 8]:
                p = peer(step)
                r = far_rows_s[0, p]
                if it == 0:
                    value = half[r]
                else:
                    value = new_duals(r, table_far[3, r]).astype(BF16)
                term_send[it, p] = dot(value, far[p]).astype(BF16)
            if it == 0 and g == 0:
                pl.semaphore_wait(barrier, NB - 1 + 2 * NS - 2)
            for i in range(g, min(g + 8, NB - 1)):
                send_term(i)
        term_recv[it, me_b] = term_send[it, me_b]

        def to_half(rb, c):
            new = new_duals(rb, table_far[3, rb])
            dual[:, pl.ds(pl.multiple_of(rb * TILE, TILE), TILE)] = new
            half[rb] = new.astype(BF16)
            return c

        if it > 0:
            lax.fori_loop(0, RB, to_half, 0, unroll=8)

        if it == 0:
            load_far_cols.wait()
            for p in range(NB):
                idx_send[p] = jnp.full((1, TILE), far_cols_s[0, p], jnp.int32)
            for step in ORDER[:-1]:
                p = peer(step)
                pltpu.make_async_remote_copy(
                    src_ref=idx_send.at[p],
                    dst_ref=idx_recv.at[me_b],
                    send_sem=idx_sem.at[0],
                    recv_sem=idx_sem.at[1],
                    device_id=(me_s, p),
                    device_id_type=MESH,
                ).start()
            load_first.wait()
            load_first_cost.wait()
            first_recv[me_s, 0:XB] = first_own[...]
            first_recv[me_s, XB : 2 * XB] = first_own_cost[...]
            first_recv[me_s, 2 * XB :] = jnp.zeros((8 - 2 * XB, TILE), F32)

            def send_first(k, c):
                pltpu.make_async_remote_copy(
                    src_ref=first_recv.at[me_s],
                    dst_ref=first_recv.at[me_s],
                    send_sem=idx_sem.at[2],
                    recv_sem=idx_sem.at[3],
                    device_id=((me_s + k) % NS, me_b),
                    device_id_type=MESH,
                ).start()
                return c

            lax.fori_loop(1, NS, send_first, 0)
            load_link_rows.wait()
            load_link_cols.wait()
            load_link.wait()

        for n in range(NK):
            link_lhs[n : n + 1, :] = jnp.sum(
                half[link_rows_s[0, n]].astype(F32), axis=0, keepdims=True
            )
        sums = link_lhs[...]
        high = sums.astype(BF16)
        low = (sums - high.astype(F32)).astype(BF16)
        lhs = jnp.concatenate([high, low], axis=0)
        block = lax.broadcasted_iota(jnp.int32, (FB, TILE), 0)
        part = jnp.zeros((FB, TILE), F32)
        for n in range(NK):
            both = dot(lhs, link[n])
            row = both[n : n + 1] + both[NK + n : NK + n + 1]
            part = part + jnp.where(block == link_cols_s[0, n], row, 0.0)
        own = me_s * 2 + mc
        z_recv[it, own] = part.astype(BF16)

        def send_z(k, c):
            z, b = group_peer(k)
            pltpu.make_async_remote_copy(
                src_ref=z_recv.at[it, own],
                dst_ref=z_recv.at[it, own],
                send_sem=sems.at[it, 1, 0],
                recv_sem=sems.at[it, 1, 1],
                device_id=(z, b),
                device_id_type=MESH,
            ).start()
            return c

        lax.fori_loop(1, 2 * NS, send_z, 0)

        if it == 0:
            for copy in to_smem:
                copy.wait()
            load_tiles.wait()

        def gradient_step(n, total):
            keep = table[2, n].astype(F32)
            total = total * keep + dot(half[table[1, n]], tiles[table[0, n]])
            run[n] = total
            return total

        lax.fori_loop(0, NL, gradient_step, zero, unroll=UNROLL)

        if it == 0:
            load_rec.wait()
            load_cost.wait()

        def base_recourse(cb, c):
            at = pl.ds(pl.multiple_of(cb * TILE, TILE), TILE)
            old = rec[:, at]
            rec_old[cb] = old
            rec_base[cb] = old - PRIMAL * (cost_v[:, at] - run[table[3, cb]])
            return c

        lax.fori_loop(0, CB, base_recourse, 0, unroll=8)

        if it == 0:

            def turn(q, c):
                far_t[q] = far[q].T
                return c

            lax.fori_loop(0, NF, turn, 0, unroll=8)

            bytes_of(idx_recv, NB - 1, idx_sem.at[1])
            idx_recv[me_b] = idx_send[me_b]
            lane = lax.broadcasted_iota(jnp.int32, (1, WF), 1)
            wanted = jnp.full((1, WF), 64, jnp.int32)
            for q in range(NB):
                wanted = jnp.where(lane == q, idx_recv[q], wanted)
            want_key = jnp.broadcast_to(wanted.astype(F32), (8, WF))
            want_tables = sorted_tables(want_key, want_key, NF, WF, NF)
            for i, value in enumerate(want_tables):
                table_want_v[i : i + 1, :] = whole(value, FAR_LIMITS[i])
            table_want_v[1:2, :] = jnp.minimum(wanted, CB - 1)
            load(table_want_v, table_want, 0).wait()

        bytes_of(z_recv.at[it], 2 * NS - 1, sems.at[it, 1, 1])
        total = z_recv[it, 0].astype(F32)
        for k in range(1, 2 * NS):
            total = total + z_recv[it, k].astype(F32)
        place = me_b // 2
        b_recv[it, place] = total.astype(BF16)
        for step in STEPS[:-1]:
            pltpu.make_async_remote_copy(
                src_ref=b_recv.at[it, place],
                dst_ref=b_recv.at[it, place],
                send_sem=sems.at[it, 3, 0],
                recv_sem=sems.at[it, 3, 1],
                device_id=(me_s, peer(step + (0,))),
                device_id_type=MESH,
            ).start()

        for i, g in enumerate(GROUPS):
            bytes_of(term_recv.at[it], len(g), sems.at[it, 0, i])

        def want_step(k, total):
            keep = table_want[2, k].astype(F32)
            total = total * keep + term_recv[it, table_want[0, k]].astype(F32)
            run_want[k] = total
            return total

        lax.fori_loop(0, NF, want_step, zero, unroll=16)

        send_col = send_all(it, col_send, col_recv, 2)
        for g in range(0, NB, 8):
            for step in ORDER[g : g + 8]:
                p = peer(step)
                w = table_want[1, p]
                col_send[it, p] = new_recourse(w, table_want[3, w])[1]
            for i in range(g, min(g + 8, NB - 1)):
                send_col(i)
        col_recv[it, me_b] = col_send[it, me_b]

        def update_recourse(cb, c):
            new, bar = new_recourse(cb, table_want[3, cb])
            bars[cb] = bar
            rec[:, pl.ds(pl.multiple_of(cb * TILE, TILE), TILE)] = new
            return c

        lax.fori_loop(0, CB, update_recourse, 0, unroll=8)
        if it == ITERS - 1:
            store_rec = pltpu.make_async_copy(rec, rec_out, out_sem.at[0])
            store_rec.start()

        def image_step(n, total):
            keep = table[6, n].astype(F32)
            total = total * keep + dot_t(bars[table[5, n]], tiles[table[4, n]])
            run[n] = total
            return total

        lax.fori_loop(0, NL, image_step, zero, unroll=UNROLL)
        if it == 0:
            load_inflow.wait()

        def base_duals(rb, c):
            at = pl.ds(pl.multiple_of(rb * TILE, TILE), TILE)
            dual_base[rb] = dual[:, at] + DUAL * (
                inflow[:, at].astype(F32) - run[table[7, rb]]
            )
            return c

        lax.fori_loop(0, RB, base_duals, 0, unroll=8)

        if it == 0:
            bytes_of(first_recv, NS - 1, idx_sem.at[3])
            for s in range(NS):
                first_full[s * XB : (s + 1) * XB, :] = first_recv[s, 0:XB]
                first_cost[s * XB : (s + 1) * XB, :] = first_recv[s, XB : 2 * XB]
        bytes_of(b_recv.at[it], NB // 2 - 1, sems.at[it, 3, 1])
        total = b_recv[it, 0].astype(F32)
        for k in range(1, NB // 2):
            total = total + b_recv[it, k].astype(F32)
        old_first = first_full[...]
        new_first = jnp.maximum(
            old_first - FIRST * (first_cost[...] - total / (S * NS)), 0.0
        )
        first_full[...] = new_first
        if it == ITERS - 1:
            for i in range(XB):
                first_own[i : i + 1, :] = first_full[pl.ds(me_s * XB + i, 1), :]
            store_first = pltpu.make_async_copy(first_own, first_out, out_sem.at[1])
            store_first.start()

        link_img[0:FB, :] = 2.0 * new_first - old_first
        for n in range(NK):
            link_lhs[n : n + 1, :] = link_img[pl.ds(link_cols_s[0, n], 1), :]
        lhs = link_lhs[...].astype(BF16)
        block = lax.broadcasted_iota(jnp.int32, (RB, TILE), 0)
        image = jnp.zeros((RB, TILE), F32)
        for n in range(NK):
            row = dot_t(lhs, link[n])[n : n + 1]
            image = image + jnp.where(block == link_rows_s[0, n], row, 0.0)
        link_img[...] = image

        product[me_b] = dot(col_recv[it, me_b], far_t[me_b])
        for i in (2, 1, 0):
            g = GROUPS[i]
            bytes_of(col_recv.at[it], len(g), sems.at[it, 2, i])
            for k in g:
                q = source(ORDER[k])
                product[q] = dot(col_recv[it, q], far_t[q])

        def far_step(k, total):
            total = total * table_far[2, k].astype(F32) + product[table_far[0, k]]
            run_far[k] = total
            return total

        lax.fori_loop(0, NF, far_step, zero, unroll=32)

    parts = []
    for part in range(2):

        def update_duals(rb, c):
            at = pl.ds(pl.multiple_of(rb * TILE, TILE), TILE)
            dual[:, at] = new_duals(rb, table_far[3, rb])
            return c

        lax.fori_loop(part * RB // 2, (part + 1) * RB // 2, update_duals, 0, unroll=10)
        at = pl.ds(part * RB // 2 * TILE, RB // 2 * TILE)
        copy = pltpu.make_async_copy(dual.at[:, at], dual_out.at[:, at], out_sem.at[2 + part])
        copy.start()
        parts.append(copy)
    bytes_of(idx_recv, NB - 1, idx_sem.at[0])
    bytes_of(first_recv, NS - 1, idx_sem.at[2])
    for it in range(ITERS):
        bytes_of(term_recv.at[it], NB - 1, sems.at[it, 0, 3])
        bytes_of(z_recv.at[it], 2 * NS - 1, sems.at[it, 1, 0])
        bytes_of(col_recv.at[it], NB - 1, sems.at[it, 2, 3])
        bytes_of(b_recv.at[it], NB // 2 - 1, sems.at[it, 3, 0])
    store_rec.wait()
    store_first.wait()
    for copy in parts:
        copy.wait()


def hand_out(first, rec, dual, first_out, rec_out, dual_out):
    first_out[...] = first[...]
    rec_out[...] = rec[...]
    dual_out[...] = dual[...]


def body(
    local_tiles,
    local_rows,
    local_cols,
    far_tiles,
    far_rows,
    far_cols,
    link_tiles,
    link_rows,
    link_cols,
    inflows,
    recourse_cost,
    first_cost,
    first_section,
    recourse,
    duals,
):
    hbm = pl.BlockSpec(memory_space=pltpu.HBM)
    dma = pltpu.SemaphoreType.DMA
    vmem, smem = pltpu.VMEM, pltpu.SMEM
    int32 = jnp.int32
    shapes = (
        jax.ShapeDtypeStruct((XB, TILE), F32),
        jax.ShapeDtypeStruct((S, CB * TILE), F32),
        jax.ShapeDtypeStruct((S, RB * TILE), F32),
    )
    results = pl.pallas_call(
        kernel,
        out_shape=shapes,
        in_specs=[hbm] * 15,
        out_specs=(hbm, hbm, hbm),
        scratch_shapes=[
            smem((1, NF), int32),
            smem((1, NF), int32),
            smem((1, NK), int32),
            smem((1, NK), int32),
            vmem((1, NL), int32),
            vmem((1, NL), int32),
            vmem((1, NF), int32),
            vmem((1, CB * TILE), F32),
            vmem((XB, TILE), F32),
            vmem((XB, TILE), F32),
            vmem((NS, 8, TILE), F32),
            vmem((FB, TILE), F32),
            vmem((FB, TILE), F32),
            vmem((NL, TILE, TILE), BF16),
            vmem((NF, TILE, TILE), BF16),
            vmem((NF, TILE, TILE), BF16),
            vmem((NK, TILE, TILE), BF16),
            vmem((S, RB * TILE), BF16),
            vmem((S, CB * TILE), F32),
            vmem((CB, S, TILE), F32),
            vmem((CB, S, TILE), F32),
            vmem((S, RB * TILE), F32),
            vmem((RB, S, TILE), F32),
            vmem((RB, S, TILE), BF16),
            vmem((CB, S, TILE), BF16),
            vmem((NL + 1, S, TILE), F32),
            vmem((NF + 1, S, TILE), F32),
            vmem((NF + 1, S, TILE), F32),
            vmem((NF, S, TILE), F32),
            vmem((NK, TILE), F32),
            vmem((RB, TILE), F32),
            vmem((8, W), int32),
            vmem((4, WF), int32),
            vmem((4, WF), int32),
            smem((8, W), int32),
            smem((4, WF), int32),
            smem((4, WF), int32),
            vmem((NB, 1, TILE), int32),
            vmem((NB, 1, TILE), int32),
            vmem((ITERS, NB, S, TILE), BF16),
            vmem((ITERS, NB, S, TILE), BF16),
            vmem((ITERS, NB, S, TILE), BF16),
            vmem((ITERS, NB, S, TILE), BF16),
            vmem((ITERS, 2 * NS, FB, TILE), BF16),
            vmem((ITERS, NB // 2, FB, TILE), BF16),
            dma((16,)),
            dma((4,)),
            dma((4,)),
            dma((ITERS, 4, 4)),
        ],
        compiler_params=pltpu.CompilerParams(
            collective_id=0, has_side_effects=True, vmem_limit_bytes=62 << 20
        ),
        name="dispatch",
    )(
        far_rows.reshape(1, NF),
        far_cols.reshape(1, NF),
        link_rows.reshape(1, NK),
        link_cols.reshape(1, NK),
        local_rows.reshape(1, NL),
        local_cols.reshape(1, NL),
        recourse_cost.reshape(1, CB * TILE),
        first_cost.reshape(XB, TILE),
        first_section.reshape(XB, TILE),
        local_tiles,
        far_tiles.reshape(NF, TILE, TILE),
        link_tiles,
        inflows,
        recourse,
        duals,
    )
    first_out, rec_out, dual_out = pl.pallas_call(
        hand_out,
        out_shape=shapes,
        in_specs=[pl.BlockSpec(memory_space=vmem)] * 3,
        out_specs=[pl.BlockSpec(memory_space=vmem)] * 3,
        compiler_params=pltpu.CompilerParams(vmem_limit_bytes=62 << 20),
        name="hand_out",
    )(*results)
    return first_out.reshape(XB * TILE), rec_out, dual_out


def solution(mesh):
    in_specs = (
        P("blk", None, None),
        P("blk"),
        P("blk"),
        P("blk", None, None, None),
        P("blk", None),
        P("blk", None),
        P(("scen", "blk"), None, None),
        P(("scen", "blk")),
        P(("scen", "blk")),
        P("scen", "blk"),
        P("blk"),
        P("scen"),
        P("scen"),
        P("scen", "blk"),
        P("scen", "blk"),
    )
    out_specs = (P("scen"), P("scen", "blk"), P("scen", "blk"))
    return jax.shard_map(body, mesh=mesh, in_specs=in_specs, out_specs=out_specs, check_vma=False)
```

time: 64.2 us -> 43.2 us (0.67)
  local copies, waits for them, and re-layouts: 13.6 us -> 0 us
  Pallas kernels: 49.4 us -> 42.5 us
    unnamed x31 -> x0, local copies, waits for them, and re-layouts: 13.6 us -> none
    pallas_call x1 -> x2, Pallas kernels: 49.4 us -> 42.5 us  [the longest x1 40.2 us: body(): pl.pallas_call(kernel, out_shape=shapes, in_specs=[hbm] * 15, out_specs=(...]
where the time goes in v2:
time: 43.2 us; the launch traced here: 43.1 us
  Pallas kernels  42.5 us (98%)
  between operations  0.64 us (1%)
    pallas_call x1, Pallas kernels, body(): pl.pallas_call(kernel, out_shape=shapes, in_specs=[hbm] * 15, out_specs=(...  40.2 us
    pallas_call x1, Pallas kernels, body(): pl.pallas_call(hand_out, out_shape=shapes, in_specs=[pl.BlockSpec(memory_...  2.3 us

profile of v2, /device:TPU:1, one launch (start us, length us, event | category | flops | bytes accessed | tf_op | source)
XLA Modules:
  0.0 43.1 jit_solution(10150606504751909364)
XLA Ops:
  0.6 40.2 %dispatch.1 = (f32[2,128]{1,0:T(2,128)}, f32[32,4096]{1,0:T(8,128)}, f32[32,5120]{1,0:T(8,128)}) custom-call(s32[1,32]{1,0:T(1,128)} %bitcast.17, s32[1,32]{1,0:T(1,128)} %bitcast.18, s32[1,16]{1,0:T(1,128)} %bitcast.19, s32[1,16]{1,0:T(1,128)} %bitcast.20, s32[1,224]{1,0:T(1,128)} %bitcast.13, s32[1,224]{1,0:T(1,128)} %bitcast.14, f32[1,4096]{1,0:T(1,128)} %bitcast.12, ...), custom_call_target="tpu_custom_call" | custom-call | tf_op jit(solution)/shard_map/dispatch/pallas_call | solution.py:572
  40.8 2.3 %hand_out.1 = (f32[2,128]{1,0:T(2,128)}, f32[32,4096]{1,0:T(8,128)}, f32[32,5120]{1,0:T(8,128)}) custom-call(f32[2,128]{1,0:T(2,128)} %get-tuple-element.9.first, f32[32,4096]{1,0:T(8,128)} %get-tuple-element.10.rec, f32[32,5120]{1,0:T(8,128)} %get-tuple-element.11.dual), custom_call_target="tpu_custom_call" | custom-call | tf_op jit(solution)/shard_map/hand_out/pallas_call | solution.py:649

commit v3 on v2

--- a/solution.py
+++ b/solution.py
@@ -30,13 +30,14 @@
     tuple(i for i in range(NB - 1) if i % 16 in part)
     for part in (range(0, 5), range(5, 11), range(11, 16))
 )
+TAKE = [NB - 1] + [i for part in GROUPS[::-1] for i in part]
 UNROLL = 56
 
 PRIMAL = 0.4
 FIRST = 2.0
 DUAL = 0.4
-LIMITS = (NL - 1, RB - 1, 1, NL, NL - 1, CB - 1, 1, NL)
-FAR_LIMITS = (NF - 1, CB - 1, 1, NF)
+COL_LIMITS = (NL - 1, RB - 1, 1, NL)
+ROW_LIMITS = (NL - 1, CB - 1, 1, NL)
 MESH = pl.DeviceIdType.MESH
 F32 = jnp.float32
 BF16 = jnp.bfloat16
@@ -52,6 +53,16 @@
 
 def whole(value, top):
     return jnp.clip(value[0:1].astype(jnp.int32), 0, top)
+
+
+def chain_tables(column, key):
+    rows = lax.broadcasted_iota(jnp.int32, (NF, WF), 0)
+    lanes = lax.broadcasted_iota(jnp.int32, (NF, WF), 1)
+    result = []
+    for hit in ((column == key) & (rows < lanes), column == lanes):
+        top = jnp.max(jnp.where(hit, rows + 1, 0), axis=0, keepdims=True)
+        result.append(jnp.where(top == 0, NF, top - 1))
+    return result
 
 
 def sorted_tables(key, other, count, width, empty):
@@ -92,15 +103,14 @@
     rec_h,
     dual_h,
     first_out,
-    rec_out,
-    dual_out,
+    rec,
+    dual,
     far_rows_s,
     far_cols_s,
     link_rows_s,
     link_cols_s,
     local_rows_v,
     local_cols_v,
-    far_rows_v,
     cost_v,
     first_own,
     first_own_cost,
@@ -112,23 +122,23 @@
     far_t,
     link,
     inflow,
-    rec,
     rec_base,
     rec_old,
-    dual,
     dual_base,
     half,
     bars,
     run,
     run_far,
     run_want,
-    product,
     link_lhs,
     link_img,
-    table_v,
+    table_col_v,
+    table_row_v,
     table_far_v,
     table_want_v,
-    table,
+    chain_v,
+    table_col,
+    table_row,
     table_far,
     table_want,
     idx_send,
@@ -140,7 +150,6 @@
     z_recv,
     b_recv,
     load_sem,
-    out_sem,
     idx_sem,
     sems,
 ):
@@ -155,6 +164,10 @@
     def source(step):
         return peer(tuple(-d for d in step))
 
+    def taken(step):
+        back = tuple(-d % n for d, n in zip(step, (4, 4, 2)))
+        return TAKE.index(ORDER.index(back))
+
     def group_peer(k):
         return (me_s + k // 2) % NS, me_b - mc + (mc + k) % 2
 
@@ -178,59 +191,36 @@
         copy.start()
         return copy
 
+    load_dual = load(dual_h, dual, 5)
+    load_far_rows = load(far_rows_h, far_rows_s, 3)
+    load_far = load(far_h, far, 6)
     load_rows = load(local_rows_h, local_rows_v, 0)
     load_cols = load(local_cols_h, local_cols_v, 1)
-    load_far_rows_v = load(far_rows_h, far_rows_v, 2)
-    load_far_rows = load(far_rows_h, far_rows_s, 3)
     load_far_cols = load(far_cols_h, far_cols_s, 4)
-    load_dual = load(dual_h, dual, 5)
-    load_far = load(far_h, far, 6)
     load_link_rows = load(link_rows_h, link_rows_s, 7)
     load_link_cols = load(link_cols_h, link_cols_s, 8)
-    load_link = load(link_h, link, 9)
     load_first = load(first_h, first_own, 10)
     load_first_cost = load(first_cost_h, first_own_cost, 11)
+
+    zero = jnp.zeros((S, TILE), F32)
+    run[NL] = zero
+    run_far[NF] = zero
+    run_want[NF] = zero
+
+    load_dual.wait()
+
+    def first_half(rb, c):
+        half[rb] = dual[:, pl.ds(pl.multiple_of(rb * TILE, TILE), TILE)].astype(BF16)
+        return c
+
+    lax.fori_loop(0, RB, first_half, 0, unroll=8)
+    load_far_rows.wait()
+    load_far.wait()
+    load_link = load(link_h, link, 9)
     load_tiles = load(local_h, tiles, 12)
     load_cost = load(cost_h, cost_v, 13)
     load_rec = load(rec_h, rec, 14)
     load_inflow = load(inflow_h, inflow, 15)
-
-    load_rows.wait()
-    load_cols.wait()
-    load_far_rows_v.wait()
-    pad = jnp.full((8, W - NL), 64.0, F32)
-    row_key = jnp.concatenate(
-        [jnp.broadcast_to(local_rows_v[...].astype(F32), (8, NL)), pad], axis=1
-    )
-    col_key = jnp.concatenate(
-        [jnp.broadcast_to(local_cols_v[...].astype(F32), (8, NL)), pad], axis=1
-    )
-    pad_far = jnp.full((8, WF - NF), 64.0, F32)
-    far_key = jnp.concatenate(
-        [jnp.broadcast_to(far_rows_v[...].astype(F32), (8, NF)), pad_far], axis=1
-    )
-    col_tables = sorted_tables(col_key, row_key, NL, W, NL)
-    row_tables = sorted_tables(row_key, col_key, NL, W, NL)
-    for i, value in enumerate(col_tables + row_tables):
-        table_v[i : i + 1, :] = whole(value, LIMITS[i])
-    far_tables = sorted_tables(far_key, far_key, NF, WF, NF)
-    for i, value in enumerate(far_tables):
-        table_far_v[i : i + 1, :] = whole(value, FAR_LIMITS[i])
-    to_smem = [load(table_v, table, 0), load(table_far_v, table_far, 1)]
-    zero = jnp.zeros((S, TILE), F32)
-    run[NL] = zero
-    run_far[NF] = zero
-    run_want[NF] = zero
-
-    load_dual.wait()
-
-    def first_half(rb, c):
-        half[rb] = dual[:, pl.ds(pl.multiple_of(rb * TILE, TILE), TILE)].astype(BF16)
-        return c
-
-    lax.fori_loop(0, RB, first_half, 0, unroll=8)
-    load_far_rows.wait()
-    load_far.wait()
 
     def send_all(it, src, dst, which):
         def one(i):
@@ -260,23 +250,24 @@
 
     for it in range(ITERS):
         send_term = send_all(it, term_send, term_recv, 0)
-        for g in range(0, NB, 8):
-            for step in ORDER[g : g + 8]:
+        width = NB if it == 0 else 8
+        for g in range(0, NB, width):
+            for step in ORDER[g : g + width]:
                 p = peer(step)
                 r = far_rows_s[0, p]
                 if it == 0:
                     value = half[r]
                 else:
-                    value = new_duals(r, table_far[3, r]).astype(BF16)
+                    value = new_duals(r, table_far[1, r]).astype(BF16)
                 term_send[it, p] = dot(value, far[p]).astype(BF16)
-            if it == 0 and g == 0:
+            if it == 0:
                 pl.semaphore_wait(barrier, NB - 1 + 2 * NS - 2)
-            for i in range(g, min(g + 8, NB - 1)):
+            for i in range(g, min(g + width, NB - 1)):
                 send_term(i)
         term_recv[it, me_b] = term_send[it, me_b]
 
         def to_half(rb, c):
-            new = new_duals(rb, table_far[3, rb])
+            new = new_duals(rb, table_far[1, rb])
             dual[:, pl.ds(pl.multiple_of(rb * TILE, TILE), TILE)] = new
             half[rb] = new.astype(BF16)
             return c
@@ -352,13 +343,25 @@
         lax.fori_loop(1, 2 * NS, send_z, 0)
 
         if it == 0:
-            for copy in to_smem:
-                copy.wait()
+            load_rows.wait()
+            load_cols.wait()
+            pad = jnp.full((8, W - NL), 64.0, F32)
+            row_key = jnp.concatenate(
+                [jnp.broadcast_to(local_rows_v[...].astype(F32), (8, NL)), pad], axis=1
+            )
+            col_key = jnp.concatenate(
+                [jnp.broadcast_to(local_cols_v[...].astype(F32), (8, NL)), pad], axis=1
+            )
+            col_tables = sorted_tables(col_key, row_key, NL, W, NL)
+            for i, value in enumerate(col_tables):
+                table_col_v[i : i + 1, :] = whole(value, COL_LIMITS[i])
+            col_to_smem = load(table_col_v, table_col, 0)
+            col_to_smem.wait()
             load_tiles.wait()
 
         def gradient_step(n, total):
-            keep = table[2, n].astype(F32)
-            total = total * keep + dot(half[table[1, n]], tiles[table[0, n]])
+            keep = table_col[2, n].astype(F32)
+            total = total * keep + dot(half[table_col[1, n]], tiles[table_col[0, n]])
             run[n] = total
             return total
 
@@ -372,7 +375,7 @@
             at = pl.ds(pl.multiple_of(cb * TILE, TILE), TILE)
             old = rec[:, at]
             rec_old[cb] = old
-            rec_base[cb] = old - PRIMAL * (cost_v[:, at] - run[table[3, cb]])
+            rec_base[cb] = old - PRIMAL * (cost_v[:, at] - run[table_col[3, cb]])
             return c
 
         lax.fori_loop(0, CB, base_recourse, 0, unroll=8)
@@ -385,18 +388,34 @@
 
             lax.fori_loop(0, NF, turn, 0, unroll=8)
 
+            row_tables = sorted_tables(row_key, col_key, NL, W, NL)
+            for i, value in enumerate(row_tables):
+                table_row_v[i : i + 1, :] = whole(value, ROW_LIMITS[i])
+            row_to_smem = load(table_row_v, table_row, 1)
+
+            lane = lax.broadcasted_iota(jnp.int32, (1, WF), 1)
+            key = jnp.full((1, WF), 64, jnp.int32)
+            for k, i in enumerate(TAKE):
+                row = jnp.full((1, WF), far_rows_s[0, source(ORDER[i])], jnp.int32)
+                chain_v[k : k + 1, :] = row
+                key = jnp.where(lane == k, row, key)
+            for i, value in enumerate(chain_tables(chain_v[...], key)):
+                table_far_v[i : i + 1, :] = value
+            far_to_smem = load(table_far_v, table_far, 2)
+
             bytes_of(idx_recv, NB - 1, idx_sem.at[1])
             idx_recv[me_b] = idx_send[me_b]
-            lane = lax.broadcasted_iota(jnp.int32, (1, WF), 1)
-            wanted = jnp.full((1, WF), 64, jnp.int32)
-            for q in range(NB):
-                wanted = jnp.where(lane == q, idx_recv[q], wanted)
-            want_key = jnp.broadcast_to(wanted.astype(F32), (8, WF))
-            want_tables = sorted_tables(want_key, want_key, NF, WF, NF)
-            for i, value in enumerate(want_tables):
-                table_want_v[i : i + 1, :] = whole(value, FAR_LIMITS[i])
-            table_want_v[1:2, :] = jnp.minimum(wanted, CB - 1)
+            key = jnp.full((1, WF), 64, jnp.int32)
+            for k, i in enumerate(TAKE):
+                row = idx_recv[source(ORDER[i])]
+                chain_v[k : k + 1, :] = row
+                key = jnp.where(lane == k, row, key)
+            for i, value in enumerate(chain_tables(chain_v[...], key)):
+                table_want_v[i : i + 1, :] = value
+            table_want_v[2:3, :] = jnp.minimum(key, CB - 1)
             load(table_want_v, table_want, 0).wait()
+            row_to_smem.wait()
+            far_to_smem.wait()
 
         bytes_of(z_recv.at[it], 2 * NS - 1, sems.at[it, 1, 1])
         total = z_recv[it, 0].astype(F32)
@@ -414,41 +433,34 @@
                 device_id_type=MESH,
             ).start()
 
-        for i, g in enumerate(GROUPS):
-            bytes_of(term_recv.at[it], len(g), sems.at[it, 0, i])
-
-        def want_step(k, total):
-            keep = table_want[2, k].astype(F32)
-            total = total * keep + term_recv[it, table_want[0, k]].astype(F32)
-            run_want[k] = total
-            return total
-
-        lax.fori_loop(0, NF, want_step, zero, unroll=16)
+        for k, i in enumerate(TAKE):
+            for j, g in enumerate(GROUPS):
+                if i == g[0]:
+                    bytes_of(term_recv.at[it], len(g), sems.at[it, 0, j])
+            term = term_recv[it, source(ORDER[i])].astype(F32)
+            run_want[k] = run_want[table_want[0, k]] + term
 
         send_col = send_all(it, col_send, col_recv, 2)
         for g in range(0, NB, 8):
             for step in ORDER[g : g + 8]:
                 p = peer(step)
-                w = table_want[1, p]
-                col_send[it, p] = new_recourse(w, table_want[3, w])[1]
+                w = table_want[2, taken(step)]
+                col_send[it, p] = new_recourse(w, table_want[1, w])[1]
             for i in range(g, min(g + 8, NB - 1)):
                 send_col(i)
         col_recv[it, me_b] = col_send[it, me_b]
 
         def update_recourse(cb, c):
-            new, bar = new_recourse(cb, table_want[3, cb])
+            new, bar = new_recourse(cb, table_want[1, cb])
             bars[cb] = bar
             rec[:, pl.ds(pl.multiple_of(cb * TILE, TILE), TILE)] = new
             return c
 
         lax.fori_loop(0, CB, update_recourse, 0, unroll=8)
-        if it == ITERS - 1:
-            store_rec = pltpu.make_async_copy(rec, rec_out, out_sem.at[0])
-            store_rec.start()
 
         def image_step(n, total):
-            keep = table[6, n].astype(F32)
-            total = total * keep + dot_t(bars[table[5, n]], tiles[table[4, n]])
+            keep = table_row[2, n].astype(F32)
+            total = total * keep + dot_t(bars[table_row[1, n]], tiles[table_row[0, n]])
             run[n] = total
             return total
 
@@ -459,7 +471,7 @@
         def base_duals(rb, c):
             at = pl.ds(pl.multiple_of(rb * TILE, TILE), TILE)
             dual_base[rb] = dual[:, at] + DUAL * (
-                inflow[:, at].astype(F32) - run[table[7, rb]]
+                inflow[:, at].astype(F32) - run[table_row[3, rb]]
             )
             return c
 
@@ -481,9 +493,7 @@
         first_full[...] = new_first
         if it == ITERS - 1:
             for i in range(XB):
-                first_own[i : i + 1, :] = first_full[pl.ds(me_s * XB + i, 1), :]
-            store_first = pltpu.make_async_copy(first_own, first_out, out_sem.at[1])
-            store_first.start()
+                first_out[i : i + 1, :] = first_full[pl.ds(me_s * XB + i, 1), :]
 
         link_img[0:FB, :] = 2.0 * new_first - old_first
         for n in range(NK):
@@ -496,34 +506,19 @@
             image = image + jnp.where(block == link_rows_s[0, n], row, 0.0)
         link_img[...] = image
 
-        product[me_b] = dot(col_recv[it, me_b], far_t[me_b])
-        for i in (2, 1, 0):
-            g = GROUPS[i]
-            bytes_of(col_recv.at[it], len(g), sems.at[it, 2, i])
-            for k in g:
-                q = source(ORDER[k])
-                product[q] = dot(col_recv[it, q], far_t[q])
-
-        def far_step(k, total):
-            total = total * table_far[2, k].astype(F32) + product[table_far[0, k]]
-            run_far[k] = total
-            return total
-
-        lax.fori_loop(0, NF, far_step, zero, unroll=32)
-
-    parts = []
-    for part in range(2):
-
-        def update_duals(rb, c):
-            at = pl.ds(pl.multiple_of(rb * TILE, TILE), TILE)
-            dual[:, at] = new_duals(rb, table_far[3, rb])
-            return c
-
-        lax.fori_loop(part * RB // 2, (part + 1) * RB // 2, update_duals, 0, unroll=10)
-        at = pl.ds(part * RB // 2 * TILE, RB // 2 * TILE)
-        copy = pltpu.make_async_copy(dual.at[:, at], dual_out.at[:, at], out_sem.at[2 + part])
-        copy.start()
-        parts.append(copy)
+        for k, i in enumerate(TAKE):
+            for j, g in enumerate(GROUPS):
+                if i == g[0]:
+                    bytes_of(col_recv.at[it], len(g), sems.at[it, 2, j])
+            q = source(ORDER[i])
+            run_far[k] = run_far[table_far[0, k]] + dot(col_recv[it, q], far_t[q])
+
+    def update_duals(rb, c):
+        at = pl.ds(pl.multiple_of(rb * TILE, TILE), TILE)
+        dual[:, at] = new_duals(rb, table_far[1, rb])
+        return c
+
+    lax.fori_loop(0, RB, update_duals, 0, unroll=10)
     bytes_of(idx_recv, NB - 1, idx_sem.at[0])
     bytes_of(first_recv, NS - 1, idx_sem.at[2])
     for it in range(ITERS):
@@ -531,16 +526,18 @@
         bytes_of(z_recv.at[it], 2 * NS - 1, sems.at[it, 1, 0])
         bytes_of(col_recv.at[it], NB - 1, sems.at[it, 2, 3])
         bytes_of(b_recv.at[it], NB // 2 - 1, sems.at[it, 3, 0])
-    store_rec.wait()
-    store_first.wait()
-    for copy in parts:
+
+
+def hand_out(first, rec, dual, first_out, rec_out, dual_out, sem):
+    copies = [
+        pltpu.make_async_copy(first, first_out, sem.at[0]),
+        pltpu.make_async_copy(rec, rec_out, sem.at[1]),
+        pltpu.make_async_copy(dual, dual_out, sem.at[2]),
+    ]
+    for copy in copies:
+        copy.start()
+    for copy in copies:
         copy.wait()
-
-
-def hand_out(first, rec, dual, first_out, rec_out, dual_out):
-    first_out[...] = first[...]
-    rec_out[...] = rec[...]
-    dual_out[...] = dual[...]
 
 
 def body(
@@ -569,11 +566,12 @@
         jax.ShapeDtypeStruct((S, CB * TILE), F32),
         jax.ShapeDtypeStruct((S, RB * TILE), F32),
     )
+    held = [vmem(shape.shape, F32) for shape in shapes]
     results = pl.pallas_call(
         kernel,
-        out_shape=shapes,
+        out_shape=held,
         in_specs=[hbm] * 15,
-        out_specs=(hbm, hbm, hbm),
+        out_specs=[pl.BlockSpec(memory_space=vmem)] * 3,
         scratch_shapes=[
             smem((1, NF), int32),
             smem((1, NF), int32),
@@ -581,7 +579,6 @@
             smem((1, NK), int32),
             vmem((1, NL), int32),
             vmem((1, NL), int32),
-            vmem((1, NF), int32),
             vmem((1, CB * TILE), F32),
             vmem((XB, TILE), F32),
             vmem((XB, TILE), F32),
@@ -593,25 +590,25 @@
             vmem((NF, TILE, TILE), BF16),
             vmem((NK, TILE, TILE), BF16),
             vmem((S, RB * TILE), BF16),
-            vmem((S, CB * TILE), F32),
             vmem((CB, S, TILE), F32),
             vmem((CB, S, TILE), F32),
-            vmem((S, RB * TILE), F32),
             vmem((RB, S, TILE), F32),
             vmem((RB, S, TILE), BF16),
             vmem((CB, S, TILE), BF16),
             vmem((NL + 1, S, TILE), F32),
             vmem((NF + 1, S, TILE), F32),
             vmem((NF + 1, S, TILE), F32),
-            vmem((NF, S, TILE), F32),
             vmem((NK, TILE), F32),
             vmem((RB, TILE), F32),
-            vmem((8, W), int32),
-            vmem((4, WF), int32),
-            vmem((4, WF), int32),
-            smem((8, W), int32),
-            smem((4, WF), int32),
-            smem((4, WF), int32),
+            vmem((4, W), int32),
+            vmem((4, W), int32),
+            vmem((2, WF), int32),
+            vmem((3, WF), int32),
+            vmem((NF, WF), int32),
+            smem((4, W), int32),
+            smem((4, W), int32),
+            smem((2, WF), int32),
+            smem((3, WF), int32),
             vmem((NB, 1, TILE), int32),
             vmem((NB, 1, TILE), int32),
             vmem((ITERS, NB, S, TILE), BF16),
@@ -622,11 +619,10 @@
             vmem((ITERS, NB // 2, FB, TILE), BF16),
             dma((16,)),
             dma((4,)),
-            dma((4,)),
             dma((ITERS, 4, 4)),
         ],
         compiler_params=pltpu.CompilerParams(
-            collective_id=0, has_side_effects=True, vmem_limit_bytes=62 << 20
+            collective_id=0, has_side_effects=True, vmem_limit_bytes=60 << 20
         ),
         name="dispatch",
     )(
@@ -650,10 +646,11 @@
         hand_out,
         out_shape=shapes,
         in_specs=[pl.BlockSpec(memory_space=vmem)] * 3,
-        out_specs=[pl.BlockSpec(memory_space=vmem)] * 3,
-        compiler_params=pltpu.CompilerParams(vmem_limit_bytes=62 << 20),
+        out_specs=(hbm, hbm, hbm),
+        scratch_shapes=[dma((3,))],
+        compiler_params=pltpu.CompilerParams(vmem_limit_bytes=60 << 20),
         name="hand_out",
-    )(*results)
+    )(*(pltpu.with_memory_space_constraint(result, vmem) for result in results))
     return first_out.reshape(XB * TILE), rec_out, dual_out
 
 

time: 43.2 us -> 40.8 us (0.944)
  Pallas kernels: 42.5 us -> 40 us
    pallas_call x1, Pallas kernels: 2.3 us -> 1.04 us  [body(): pl.pallas_call(hand_out, out_shape=shapes, in_specs=[pl.BlockSpec(memory_...]
    pallas_call x1, Pallas kernels: 40.2 us -> 39 us  [body(): pl.pallas_call(kernel, out_shape=held, in_specs=[hbm] * 15, out_specs=[pl...]
where the time goes in v3:
time: 40.8 us; the launch traced here: 40.7 us
  Pallas kernels  40 us (98%)
  between operations  0.64 us (2%)
    pallas_call x1, Pallas kernels, body(): pl.pallas_call(kernel, out_shape=held, in_specs=[hbm] * 15, out_specs=[pl...  39 us
    pallas_call x1, Pallas kernels, body(): pl.pallas_call(hand_out, out_shape=shapes, in_specs=[pl.BlockSpec(memory_...  1.04 us

profile of v3, /device:TPU:1, one launch (start us, length us, event | category | flops | bytes accessed | tf_op | source)
XLA Modules:
  0.0 40.7 jit_solution(9289042604149460907)
XLA Ops:
  0.6 39.0 %dispatch.1 = (f32[2,128]{1,0:T(2,128)S(1)}, f32[32,4096]{1,0:T(8,128)S(1)}, f32[32,5120]{1,0:T(8,128)S(1)}) custom-call(s32[1,32]{1,0:T(1,128)} %bitcast.17, s32[1,32]{1,0:T(1,128)} %bitcast.18, s32[1,16]{1,0:T(1,128)} %bitcast.19, s32[1,16]{1,0:T(1,128)} %bitcast.20, s32[1,224]{1,0:T(1,128)} %bitcast.13, s32[1,224]{1,0:T(1,128)} %bitcast.14, ...), custom_call_target="tpu_custom_call" | custom-call | tf_op jit(solution)/shard_map/dispatch/pallas_call | solution.py:570
  39.6 1.0 %hand_out.1 = (f32[2,128]{1,0:T(2,128)}, f32[32,4096]{1,0:T(8,128)}, f32[32,5120]{1,0:T(8,128)}) custom-call(f32[2,128]{1,0:T(2,128)S(1)} %get-tuple-element.9.first, f32[32,4096]{1,0:T(8,128)S(1)} %get-tuple-element.10.rec, f32[32,5120]{1,0:T(8,128)S(1)} %get-tuple-element.11.dual), custom_call_target="tpu_custom_call" | custom-call | tf_op jit(solution)/shard_map/hand_out/pallas_call | solution.py:645

commit v4 on v3

--- a/solution.py
+++ b/solution.py
@@ -118,6 +118,7 @@
     first_full,
     first_cost,
     tiles,
+    tiles_t,
     far,
     far_t,
     link,
@@ -261,34 +262,25 @@
                     value = new_duals(r, table_far[1, r]).astype(BF16)
                 term_send[it, p] = dot(value, far[p]).astype(BF16)
             if it == 0:
+                load_far_cols.wait()
+                for p in range(NB):
+                    idx_send[p] = jnp.full((1, TILE), far_cols_s[0, p], jnp.int32)
                 pl.semaphore_wait(barrier, NB - 1 + 2 * NS - 2)
+                for step in ORDER[:-1]:
+                    p = peer(step)
+                    pltpu.make_async_remote_copy(
+                        src_ref=idx_send.at[p],
+                        dst_ref=idx_recv.at[me_b],
+                        send_sem=idx_sem.at[0],
+                        recv_sem=idx_sem.at[1],
+                        device_id=(me_s, p),
+                        device_id_type=MESH,
+                    ).start()
             for i in range(g, min(g + width, NB - 1)):
                 send_term(i)
         term_recv[it, me_b] = term_send[it, me_b]
 
-        def to_half(rb, c):
-            new = new_duals(rb, table_far[1, rb])
-            dual[:, pl.ds(pl.multiple_of(rb * TILE, TILE), TILE)] = new
-            half[rb] = new.astype(BF16)
-            return c
-
-        if it > 0:
-            lax.fori_loop(0, RB, to_half, 0, unroll=8)
-
-        if it == 0:
-            load_far_cols.wait()
-            for p in range(NB):
-                idx_send[p] = jnp.full((1, TILE), far_cols_s[0, p], jnp.int32)
-            for step in ORDER[:-1]:
-                p = peer(step)
-                pltpu.make_async_remote_copy(
-                    src_ref=idx_send.at[p],
-                    dst_ref=idx_recv.at[me_b],
-                    send_sem=idx_sem.at[0],
-                    recv_sem=idx_sem.at[1],
-                    device_id=(me_s, p),
-                    device_id_type=MESH,
-                ).start()
+        if it == 0:
             load_first.wait()
             load_first_cost.wait()
             first_recv[me_s, 0:XB] = first_own[...]
@@ -312,9 +304,12 @@
             load_link.wait()
 
         for n in range(NK):
-            link_lhs[n : n + 1, :] = jnp.sum(
-                half[link_rows_s[0, n]].astype(F32), axis=0, keepdims=True
-            )
+            r = link_rows_s[0, n]
+            if it == 0:
+                value = half[r]
+            else:
+                value = new_duals(r, table_far[1, r]).astype(BF16)
+            link_lhs[n : n + 1, :] = jnp.sum(value.astype(F32), axis=0, keepdims=True)
         sums = link_lhs[...]
         high = sums.astype(BF16)
         low = (sums - high.astype(F32)).astype(BF16)
@@ -341,6 +336,15 @@
             return c
 
         lax.fori_loop(1, 2 * NS, send_z, 0)
+
+        def to_half(rb, c):
+            new = new_duals(rb, table_far[1, rb])
+            dual[:, pl.ds(pl.multiple_of(rb * TILE, TILE), TILE)] = new
+            half[rb] = new.astype(BF16)
+            return c
+
+        if it > 0:
+            lax.fori_loop(0, RB, to_half, 0, unroll=8)
 
         if it == 0:
             load_rows.wait()
@@ -413,9 +417,7 @@
             for i, value in enumerate(chain_tables(chain_v[...], key)):
                 table_want_v[i : i + 1, :] = value
             table_want_v[2:3, :] = jnp.minimum(key, CB - 1)
-            load(table_want_v, table_want, 0).wait()
-            row_to_smem.wait()
-            far_to_smem.wait()
+            want_to_smem = load(table_want_v, table_want, 0)
 
         bytes_of(z_recv.at[it], 2 * NS - 1, sems.at[it, 1, 1])
         total = z_recv[it, 0].astype(F32)
@@ -433,6 +435,8 @@
                 device_id_type=MESH,
             ).start()
 
+        if it == 0:
+            want_to_smem.wait()
         for k, i in enumerate(TAKE):
             for j, g in enumerate(GROUPS):
                 if i == g[0]:
@@ -458,9 +462,17 @@
 
         lax.fori_loop(0, CB, update_recourse, 0, unroll=8)
 
+        if it == 0:
+            row_to_smem.wait()
+            far_to_smem.wait()
         def image_step(n, total):
             keep = table_row[2, n].astype(F32)
-            total = total * keep + dot_t(bars[table_row[1, n]], tiles[table_row[0, n]])
+            if it == 0:
+                tile = tiles[table_row[0, n]].T
+                tiles_t[n] = tile
+            else:
+                tile = tiles_t[n]
+            total = total * keep + dot(bars[table_row[1, n]], tile)
             run[n] = total
             return total
 
@@ -585,6 +597,7 @@
             vmem((NS, 8, TILE), F32),
             vmem((FB, TILE), F32),
             vmem((FB, TILE), F32),
+            vmem((NL, TILE, TILE), BF16),
             vmem((NL, TILE, TILE), BF16),
             vmem((NF, TILE, TILE), BF16),
             vmem((NF, TILE, TILE), BF16),

time: 40.8 us -> 39.7 us (0.973)
  Pallas kernels: 40 us -> 39 us
    pallas_call x1, Pallas kernels: 39 us -> 38 us  [body(): pl.pallas_call(kernel, out_shape=held, in_specs=[hbm] * 15, out_specs=[pl...]
where the time goes in v4:
time: 39.7 us; the launch traced here: 39.6 us
  Pallas kernels  39 us (98%)
  between operations  0.64 us (2%)
    pallas_call x1, Pallas kernels, body(): pl.pallas_call(kernel, out_shape=held, in_specs=[hbm] * 15, out_specs=[pl...  38 us
    pallas_call x1, Pallas kernels, body(): pl.pallas_call(hand_out, out_shape=shapes, in_specs=[pl.BlockSpec(memory_...  1.04 us

profile of v4, /device:TPU:1, one launch (start us, length us, event | category | flops | bytes accessed | tf_op | source)
XLA Modules:
  0.0 39.6 jit_solution(17502425599336513797)
XLA Ops:
  0.6 38.0 %dispatch.1 = (f32[2,128]{1,0:T(2,128)S(1)}, f32[32,4096]{1,0:T(8,128)S(1)}, f32[32,5120]{1,0:T(8,128)S(1)}) custom-call(s32[1,32]{1,0:T(1,128)} %bitcast.17, s32[1,32]{1,0:T(1,128)} %bitcast.18, s32[1,16]{1,0:T(1,128)} %bitcast.19, s32[1,16]{1,0:T(1,128)} %bitcast.20, s32[1,224]{1,0:T(1,128)} %bitcast.13, s32[1,224]{1,0:T(1,128)} %bitcast.14, ...), custom_call_target="tpu_custom_call" | custom-call | tf_op jit(solution)/shard_map/dispatch/pallas_call | solution.py:582
  38.6 1.0 %hand_out.1 = (f32[2,128]{1,0:T(2,128)}, f32[32,4096]{1,0:T(8,128)}, f32[32,5120]{1,0:T(8,128)}) custom-call(f32[2,128]{1,0:T(2,128)S(1)} %get-tuple-element.9.first, f32[32,4096]{1,0:T(8,128)S(1)} %get-tuple-element.10.rec, f32[32,5120]{1,0:T(8,128)S(1)} %get-tuple-element.11.dual), custom_call_target="tpu_custom_call" | custom-call | tf_op jit(solution)/shard_map/hand_out/pallas_call | solution.py:658

commit v5 on v4

--- a/solution.py
+++ b/solution.py
@@ -177,15 +177,15 @@
     def greet(step):
         pl.semaphore_signal(barrier, inc=1, device_id=(me_s, peer(step)), device_id_type=MESH)
 
+    def greet_z(k):
+        z, b = group_peer(k)
+        pl.semaphore_signal(barrier, inc=1, device_id=(z, b), device_id_type=MESH)
+
+    for k in sorted(range(2, 2 * NS), key=lambda k: -min(k // 2, NS - k // 2)):
+        greet_z(k)
+
     for step in ORDER[:-1]:
         greet(step)
-
-    def greet_z(k, c):
-        z, b = group_peer(k)
-        pl.semaphore_signal(barrier, inc=1, device_id=(z, b), device_id_type=MESH)
-        return c
-
-    lax.fori_loop(2, 2 * NS, greet_z, 0)
 
     def load(src, dst, i):
         copy = pltpu.make_async_copy(src, dst, load_sem.at[i])
@@ -323,7 +323,7 @@
         own = me_s * 2 + mc
         z_recv[it, own] = part.astype(BF16)
 
-        def send_z(k, c):
+        def send_z(k):
             z, b = group_peer(k)
             pltpu.make_async_remote_copy(
                 src_ref=z_recv.at[it, own],
@@ -333,9 +333,9 @@
                 device_id=(z, b),
                 device_id_type=MESH,
             ).start()
-            return c
-
-        lax.fori_loop(1, 2 * NS, send_z, 0)
+
+        for k in sorted(range(1, 2 * NS), key=lambda k: -min(k // 2, NS - k // 2)):
+            send_z(k)
 
         def to_half(rb, c):
             new = new_duals(rb, table_far[1, rb])

time: 39.7 us -> 39.4 us (level)
  Pallas kernels: 39 us -> 38.6 us
where the time goes in v5:
time: 39.4 us; the launch traced here: 39.3 us
  Pallas kernels  38.6 us (98%)
  between operations  0.64 us (2%)
    pallas_call x1, Pallas kernels, body(): pl.pallas_call(kernel, out_shape=held, in_specs=[hbm] * 15, out_specs=[pl...  37.6 us
    pallas_call x1, Pallas kernels, body(): pl.pallas_call(hand_out, out_shape=shapes, in_specs=[pl.BlockSpec(memory_...  1.04 us

profile of v5, /device:TPU:1, one launch (start us, length us, event | category | flops | bytes accessed | tf_op | source)
XLA Modules:
  0.0 39.3 jit_solution(8061551651423860715)
XLA Ops:
  0.6 37.6 %dispatch.1 = (f32[2,128]{1,0:T(2,128)S(1)}, f32[32,4096]{1,0:T(8,128)S(1)}, f32[32,5120]{1,0:T(8,128)S(1)}) custom-call(s32[1,32]{1,0:T(1,128)} %bitcast.17, s32[1,32]{1,0:T(1,128)} %bitcast.18, s32[1,16]{1,0:T(1,128)} %bitcast.19, s32[1,16]{1,0:T(1,128)} %bitcast.20, s32[1,224]{1,0:T(1,128)} %bitcast.13, s32[1,224]{1,0:T(1,128)} %bitcast.14, ...), custom_call_target="tpu_custom_call" | custom-call | tf_op jit(solution)/shard_map/dispatch/pallas_call | solution.py:582
  38.2 1.0 %hand_out.1 = (f32[2,128]{1,0:T(2,128)}, f32[32,4096]{1,0:T(8,128)}, f32[32,5120]{1,0:T(8,128)}) custom-call(f32[2,128]{1,0:T(2,128)S(1)} %get-tuple-element.9.first, f32[32,4096]{1,0:T(8,128)S(1)} %get-tuple-element.10.rec, f32[32,5120]{1,0:T(8,128)S(1)} %get-tuple-element.11.dual), custom_call_target="tpu_custom_call" | custom-call | tf_op jit(solution)/shard_map/hand_out/pallas_call | solution.py:658
